TPU v7x, 512 devices: a whole 4x8x8 slice. The times are simulated.
512 devices in a mesh: wide: 64 (over z, y_hi, x), narrow: 8 (over y_lo, core).
Axes of the slice: x: 4, y: 8 (y_hi: 2, y_lo: 4; y = y_hi * 4 + y_lo), z: 8, core: 2. Of those that a mesh axis runs over, the one named last changes fastest.
Arguments:
- fine_field: float32 [256, 16, 32, 128], P('wide', 'narrow'), may hold values from -2.5 to 2.5
- fine_counts: int32 [256, 16, 128], P('wide', 'narrow'), may hold values from 1 to 8
- fine_offset: float32 [256, 16, 128], P('wide', 'narrow'), may hold values from 0.3 to 1.8
- kriging: float32 [256, 16, 128, 896], P('wide', 'narrow'), may hold values from -0.1875 to 0.1875
- whiten: float32 [256, 16, 128, 128], P('wide', 'narrow'), may hold values from -2 to 2
- neighbours: int32 [256, 16, 4], P('wide', 'narrow'), may hold values from 0 to 4095, as said below
- coarse_list: int32 [256, 16, 3], P('wide', 'narrow'), may hold values from 0 to 127, as said below
- coarse_field: float32 [128, 32, 128], P('wide'), may hold values from -2.5 to 2.5
- coarse_counts: int32 [128, 128], P('wide'), may hold values from 1 to 8
- coarse_offset: float32 [128, 128], P('wide'), may hold values from 0.3 to 1.8
- coarse_whiten: float32 [128, 128, 128], P('wide'), may hold values from -2 to 2
- coarse_home: int32 [128], replicated, may hold values from 0 to 127, each once
Outputs:
- fine_grad: float32 [256, 16, 32, 128], P('wide', 'narrow')
- coarse_grad: float32 [128, 32, 128], P('wide')
Inputs may be any that keep to these rules, and one draw needn't show every extreme that they name: `neighbours`: entry [a, b, k] is the number of one of the eight blocks around block (a, b): rows a - 1, a or a + 1 modulo 256, columns b - 1, b or b + 1 modulo 16, not the block itself; the 4 entries of a block differ. `coarse_list`: the 3 entries of a fine block are different coarse block numbers.
All inputs are finite; a program needn't handle non-finite values.
Results may differ from a plain program's by a relative error of at most 0.0001.
Values sent between devices are 32-bit elements; how exact they have to be, the bound alone decides.
A program may use at most 64 MiB of HBM per device.

v0:
```python
import jax
import jax.numpy as jnp
from jax import lax
from jax.sharding import PartitionSpec as P

STEP_ROWS = (-1, -1, -1, 0, 0, 1, 1, 1)
STEP_COLS = (-1, 0, 1, -1, 1, -1, 0, 1)
SHAPE_K = 1.25
EXACT = lax.Precision.HIGHEST


def extended(array, sides, width):
    for axis, dim in sides:
        size, length = (lax.axis_size(axis), array.shape[dim])
        up = [(i, (i + 1) % size) for i in range(size)]
        down = [(j, i) for i, j in up]
        last = lax.slice_in_dim(array, length - width, length, axis=dim)
        initial = lax.slice_in_dim(array, 0, width, axis=dim)
        before = lax.ppermute(last, axis, up)
        after = lax.ppermute(initial, axis, down)
        array = jnp.concatenate([before, array, after], axis=dim)
    return array


def weibull_grad(field, counts, offset):
    log_counts = jnp.log(counts.astype(jnp.float32))
    return SHAPE_K * (
        jnp.exp(SHAPE_K * (log_counts[..., None, :] - offset[..., None, :] - field)) - 1.0
    )


def per_device(
    fine_field,
    fine_counts,
    fine_offset,
    kriging,
    whiten,
    neighbours,
    coarse_list,
    coarse_field,
    coarse_counts,
    coarse_offset,
    coarse_whiten,
    coarse_home,
):
    rows_here, cols_here, chain_count, site_count = fine_field.shape
    wide_count = lax.axis_size("wide")
    narrow_count = lax.axis_size("narrow")
    grid_rows = rows_here * wide_count
    grid_cols = cols_here * narrow_count
    first_row = lax.axis_index("wide") * rows_here
    first_col = lax.axis_index("narrow") * cols_here
    near_count = neighbours.shape[2]
    far_count = coarse_list.shape[2]
    joined_blocks = near_count + far_count
    owned = coarse_field.shape[0]
    coarse_total = owned * wide_count
    padded = extended(fine_field, (("wide", 0), ("narrow", 1)), 1)
    local_rows = jnp.arange(rows_here, dtype=jnp.int32)
    local_cols = jnp.arange(cols_here, dtype=jnp.int32)
    place_rows = jnp.array(STEP_ROWS, dtype=jnp.int32)
    place_cols = jnp.array(STEP_COLS, dtype=jnp.int32)
    target_rows = (first_row + local_rows[:, None, None] + place_rows[None, None, :]) % grid_rows
    target_cols = (first_col + local_cols[None, :, None] + place_cols[None, None, :]) % grid_cols
    target = target_rows * grid_cols + target_cols
    near_pick = (neighbours[:, :, :, None] == target[:, :, None, :]).astype(jnp.float32)
    storage_ids = jnp.arange(coarse_total, dtype=jnp.int32)
    by_number = (coarse_list[..., None] == storage_ids).astype(jnp.int32)
    stored_rows = jnp.sum(by_number * coarse_home, axis=-1)
    far_pick = (stored_rows[..., None] == storage_ids).astype(jnp.float32)
    window = far_pick
    far_vals = jnp.einsum(
        "ijkn,ncs->ijkcs",
        window,
        lax.all_gather(coarse_field, "wide", axis=0, tiled=True),
        precision=EXACT,
    )
    stencil = jnp.stack(
        [
            padded[1 + step_r : 1 + step_r + rows_here, 1 + step_c : 1 + step_c + cols_here]
            for step_r, step_c in zip(STEP_ROWS, STEP_COLS)
        ]
    )
    near_vals = jnp.einsum("ijkp,pijcs->ijkcs", near_pick, stencil, precision=EXACT)
    condition = jnp.concatenate([near_vals, far_vals], axis=2)
    weights = kriging.reshape(rows_here, cols_here, site_count, joined_blocks, site_count)
    predicted = jnp.einsum("ijkcm,ijskm->ijcs", condition, weights, precision=EXACT)
    residual = fine_field - predicted
    whitened = jnp.einsum("ijcs,ijts->ijct", residual, whiten, precision=EXACT)
    back_white = jnp.einsum("ijct,ijts->ijcs", whitened, whiten, precision=EXACT)
    handed_back = jnp.einsum("ijcs,ijskm->ijkcm", back_white, weights, precision=EXACT)
    spread = jnp.einsum(
        "ijkp,ijkcs->pijcs", near_pick, handed_back[:, :, :near_count], precision=EXACT
    )
    rim_terms = jnp.zeros((rows_here + 2, cols_here + 2, chain_count, site_count), jnp.float32)
    for place, (step_r, step_c) in enumerate(zip(STEP_ROWS, STEP_COLS)):
        rim_terms = rim_terms.at[
            1 + step_r : 1 + step_r + rows_here, 1 + step_c : 1 + step_c + cols_here
        ].add(spread[place])
    incoming = extended(rim_terms, (("wide", 0), ("narrow", 1)), 1)
    gradient = rim_terms[1:-1, 1:-1]
    gradient = gradient.at[rows_here - 1].add(incoming[rows_here + 3, 2 : cols_here + 2])
    gradient = gradient.at[0].add(incoming[0, 2 : cols_here + 2])
    gradient = gradient.at[:, cols_here - 1].add(incoming[2 : rows_here + 2, cols_here + 3])
    gradient = gradient.at[:, 0].add(incoming[2 : rows_here + 2, 0])
    gradient = gradient.at[rows_here - 1, cols_here - 1].add(incoming[rows_here + 3, cols_here + 3])
    gradient = gradient.at[rows_here - 1, 0].add(incoming[rows_here + 3, 0])
    gradient = gradient.at[0, cols_here - 1].add(incoming[0, cols_here + 3])
    gradient = gradient.at[0, 0].add(incoming[0, 0])
    fine_grad = weibull_grad(fine_field, fine_counts, fine_offset) - back_white + gradient
    far_back = handed_back[:, :, near_count:]
    window = far_pick
    owned_sum = lax.psum_scatter(
        jnp.einsum("ijkn,ijkcs->ncs", window, far_back, precision=EXACT),
        "wide",
        scatter_dimension=0,
        tiled=True,
    )
    owned_sum = lax.psum(owned_sum, "narrow")
    whitened_far = jnp.einsum("ncs,nts->nct", coarse_field, coarse_whiten, precision=EXACT)
    prior_far = jnp.einsum("nct,nts->ncs", whitened_far, coarse_whiten, precision=EXACT)
    coarse_grad = weibull_grad(coarse_field, coarse_counts, coarse_offset) - prior_far + owned_sum
    return (fine_grad, coarse_grad)


def solution(mesh):
    return jax.shard_map(
        per_device,
        mesh=mesh,
        in_specs=(
            P("wide", "narrow", None, None),
            P("wide", "narrow", None),
            P("wide", "narrow", None),
            P("wide", "narrow", None, None),
            P("wide", "narrow", None, None),
            P("wide", "narrow", None),
            P("wide", "narrow", None),
            P("wide", None, None),
            P("wide", None),
            P("wide", None),
            P("wide", None, None),
            P(),
        ),
        out_specs=(P("wide", "narrow", None, None), P("wide", None, None)),
        check_vma=False,
    )
```

profile of v0, /device:TPU:1, one launch (start us, length us, event | category | flops | bytes accessed | tf_op | source)
XLA Modules:
  0.0 642.2 jit_solution(6781656349382683077)
XLA Ops:
  7.2 0.0 copy-start
  7.2 0.0 all-gather.2.cloned.1.call-start
  7.2 0.7 all-gather.2.cloned.1.call-update
  7.9 0.0 reduce-scatter.2.cloned.1.call-start
  8.0 0.8 fusion.53
  8.7 3.9 collective-permute-start
  12.7 16.9 %collective-permute-start.1 = (f32[1,2,32,128]{3,2,1,0:T(8,128)S(1)}, f32[1,2,32,128]{3,2,1,0:T(8,128)S(1)}, u32[]{:S(2)}, u32[]{:S(2)}) collective-permute-start(f32[1,2,32,128]{3,2,1,0:T(8,128)S(1)} %get-tuple-element.212), channel_id=1, source_target_pairs={{8,0},{16,8},{24,16},{32,24},{40,32},{48,40},{56,48},{64,56},{72,6... | collective-permute-start | bytes 98312 | tf_op jit(solution)/shard_map/ppermute | solution.py:20
  29.6 0.7 copy.50
  30.3 1.4 and_reduce_fusion
  31.7 0.9 select_reduce_fusion
  32.6 0.7 and_select_fusion
  33.4 0.7 fusion.48
  34.1 0.1 fusion.41
  34.2 0.7 log_subtract_fusion
  34.9 1.2 fusion.58
  36.1 0.7 fusion.54
  36.8 0.0 copy-start.2
  36.8 4.6 copy.53
  41.5 0.0 copy-start.5
  41.5 0.0 collective-permute-done
  41.5 0.0 collective-permute-done.1
  41.5 0.0 copy-done.2
  41.6 3.1 collective-permute-start.2
  44.7 1.9 collective-permute-start.3
  46.6 0.6 fusion.55
  47.2 0.0 collective-permute-done.2
  47.2 3.8 collective-permute-done.3
  51.0 0.1 pad_maximum_fusion.4
  51.1 1.6 stack.35
  52.8 0.0 copy-done.5
  52.8 0.6 fusion.35
  53.4 94.2 %all-gather.2.cloned.1.call-done = f32[128,32,128]{2,1,0:T(8,128)} async-done(((f32[2,32,128]{2,1,0:T(8,128)}), f32[128,32,128]{2,1,0:T(8,128)}) %all-gather.2.cloned.1.call-update) | async-done | bytes 2097168 | tf_op jit(solution)/shard_map/all_gather | solution.py:75
  147.6 3.7 fusion
  151.3 0.2 pad_maximum_fusion
  151.6 0.0 copy-done.1
  151.6 2.3 fusion.2
  153.9 0.0 copy-done
  153.9 0.9 fusion.56
  154.8 0.6 fusion.57
  155.4 3.9 convolution_bitcast_fusion.1
  159.3 1.0 fusion.5
  160.3 0.2 copy.84
  160.5 1.2 convolution_bitcast_fusion
  161.7 2.6 copy.60
  164.3 0.0 reduce-scatter.2.cloned.1.call-update
  164.4 1.4 fusion.24
  165.7 2.0 fusion.8
  167.9 5.4 collective-permute-start.4
  173.4 1.9 collective-permute-start.5
  175.3 0.0 copy-done.6
  175.3 0.0 copy-done.7
  175.3 0.0 collective-permute-done.4
  175.4 11.1 %collective-permute-done.5 = f32[1,4,32,128]{3,2,1,0:T(8,128)S(1)} collective-permute-done((f32[1,4,32,128]{3,2,1,0:T(8,128)S(1)}, f32[1,4,32,128]{3,2,1,0:T(8,128)S(1)}, u32[]{:S(2)}, u32[]{:S(2)}) %collective-permute-start.5) | collective-permute-done | bytes 65568 | tf_op jit(solution)/shard_map/ppermute | solution.py:19
  186.5 8.1 %collective-permute-start.6 = (f32[8,1,32,128]{3,2,1,0:T(8,128)S(1)}, f32[8,1,32,128]{3,2,1,0:T(8,128)S(1)}, u32[]{:S(2)}, u32[]{:S(2)}) collective-permute-start(f32[8,1,32,128]{3,2,1,0:T(8,128)S(1)} %get-tuple-element.195), channel_id=1, source_target_pairs={{1,0},{2,1},{3,2},{4,3},{5,4},{6,5},{7,6},{0,7},{9,8},{10,9},{11,1... | collective-permute-start | bytes 393224 | tf_op jit(solution)/shard_map/ppermute | solution.py:20
  194.6 5.3 collective-permute-start.7
  200.0 1.1 collective-permute-done.6
  201.1 1.0 collective-permute-done.7
  202.1 1.3 fusion.31
  203.5 0.7 subtract_add_fusion
  204.2 355.1 %reduce-scatter.2.cloned.1.call-done = f32[2,32,128]{2,1,0:T(8,128)} async-done(((f32[128,32,128]{2,1,0:T(8,128)}), f32[2,32,128]{2,1,0:T(8,128)}) %reduce-scatter.2.cloned.1.call-update) | async-done | bytes 32784 | tf_op jit(solution)/shard_map/reduce_scatter | solution.py:113
  559.2 75.3 %psum.7 = f32[2,32,128]{2,1,0:T(8,128)S(1)} all-reduce(f32[2,32,128]{2,1,0:T(8,128)} %reduce-scatter.2.cloned.1.call-done), channel_id=1, replica_groups=mesh['wide'=64,'narrow'=8] {'narrow'}, use_global_device_ids=true, to_apply=%region_3.4 | all-reduce | flops 8192 | bytes 65536 | tf_op jit(solution)/shard_map/psum | solution.py:119
  634.5 0.0 copy-done.3
  634.5 0.0 copy-done.4
  634.5 0.8 fusion.3
  (34 shorter events, 0.5 us)
Async XLA Ops:
  7.2 146.7 %copy-start = (f32[4,2,128,128]{3,2,1,0:T(8,128)S(1)}, f32[4,2,128,128]{3,2,1,0:T(8,128)}, u32[]{:S(2)}) copy-start(f32[4,2,128,128]{3,2,1,0:T(8,128)} %param.50) | copy-start | bytes 1572868
  7.2 140.4 %all-gather.2.cloned.1.call-start = ((), (), s32[]{:S(2)}) async-start(), calls=%async_computation.1 | async-start | bytes 2129920 | tf_op jit(solution)/shard_map/all_gather | solution.py:75
  7.9 551.3 %reduce-scatter.2.cloned.1.call-start = ((), (), s32[]{:S(2)}) async-start(), calls=%async_computation.2 | async-start | bytes 2129920 | tf_op jit(solution)/shard_map/reduce_scatter | solution.py:113
  8.7 32.7 %collective-permute-start = (f32[1,2,32,128]{3,2,1,0:T(8,128)S(1)}, f32[1,2,32,128]{3,2,1,0:T(8,128)S(1)}, u32[]{:S(2)}, u32[]{:S(2)}) collective-permute-start(f32[1,2,32,128]{3,2,1,0:T(8,128)S(1)} %get-tuple-element.213), channel_id=1, source_target_pairs={{0,8},{8,16},{16,24},{24,32},{32,40},{40,48},{48,56},{56,64},{64,7... | collective-permute-start | bytes 98312 | tf_op jit(solution)/shard_map/ppermute | solution.py:19
  12.7 28.8 %collective-permute-start.1 = (f32[1,2,32,128]{3,2,1,0:T(8,128)S(1)}, f32[1,2,32,128]{3,2,1,0:T(8,128)S(1)}, u32[]{:S(2)}, u32[]{:S(2)}) collective-permute-start(f32[1,2,32,128]{3,2,1,0:T(8,128)S(1)} %get-tuple-element.212), channel_id=1, source_target_pairs={{8,0},{16,8},{24,16},{32,24},{40,32},{48,40},{56,48},{64,56},{72,6... | collective-permute-start | bytes 98312 | tf_op jit(solution)/shard_map/ppermute | solution.py:20
  36.8 4.7 copy-start.2
  41.5 11.3 %copy-start.5 = (s32[4,2,4]{2,1,0:T(2,128)S(1)}, s32[4,2,4]{2,1,0:T(2,128)}, u32[]{:S(2)}) copy-start(s32[4,2,4]{2,1,0:T(2,128)} %param.51) | copy-start | bytes 388
  41.6 5.7 collective-permute-start.2
  44.7 6.3 collective-permute-start.3
  147.6 4.0 copy-start.1
  164.3 11.0 %copy-start.6 = (f32[2,128]{1,0:T(2,128)S(1)}, f32[2,128]{1,0:T(2,128)}, u32[]{:S(2)}) copy-start(f32[2,128]{1,0:T(2,128)} %param.55) | copy-start | bytes 3076
  164.3 11.0 %copy-start.7 = (s32[2,128]{1,0:T(2,128)S(1)}, s32[2,128]{1,0:T(2,128)}, u32[]{:S(2)}) copy-start(s32[2,128]{1,0:T(2,128)} %param.54) | copy-start | bytes 3076
  164.3 470.2 %copy-start.3 = (f32[2,128,128]{2,1,0:T(8,128)S(1)}, f32[2,128,128]{2,1,0:T(8,128)}, u32[]{:S(2)}) copy-start(f32[2,128,128]{2,1,0:T(8,128)} %param.56) | copy-start | bytes 393220
  164.3 470.2 %copy-start.4 = (f32[2,32,128]{2,1,0:T(8,128)S(1)}, f32[2,32,128]{2,1,0:T(8,128)}, u32[]{:S(2)}) copy-start(f32[2,32,128]{2,1,0:T(8,128)} %param.53) | copy-start | bytes 98308
  167.9 7.4 %collective-permute-start.4 = (f32[1,4,32,128]{3,2,1,0:T(8,128)S(1)}, f32[1,4,32,128]{3,2,1,0:T(8,128)S(1)}, u32[]{:S(2)}, u32[]{:S(2)}) collective-permute-start(f32[1,4,32,128]{3,2,1,0:T(8,128)S(1)} %get-tuple-element.197), channel_id=1, source_target_pairs={{8,0},{16,8},{24,16},{32,24},{40,32},{48,40},{56,48},{64,56},{72,6... | collective-permute-start | bytes 196616 | tf_op jit(solution)/shard_map/ppermute | solution.py:20
  173.4 13.1 %collective-permute-start.5 = (f32[1,4,32,128]{3,2,1,0:T(8,128)S(1)}, f32[1,4,32,128]{3,2,1,0:T(8,128)S(1)}, u32[]{:S(2)}, u32[]{:S(2)}) collective-permute-start(f32[1,4,32,128]{3,2,1,0:T(8,128)S(1)} %get-tuple-element.196), channel_id=1, source_target_pairs={{0,8},{8,16},{16,24},{24,32},{32,40},{40,48},{48,56},{56,64},{64,7... | collective-permute-start | bytes 196616 | tf_op jit(solution)/shard_map/ppermute | solution.py:19
  186.5 14.5 %collective-permute-start.6 = (f32[8,1,32,128]{3,2,1,0:T(8,128)S(1)}, f32[8,1,32,128]{3,2,1,0:T(8,128)S(1)}, u32[]{:S(2)}, u32[]{:S(2)}) collective-permute-start(f32[8,1,32,128]{3,2,1,0:T(8,128)S(1)} %get-tuple-element.195), channel_id=1, source_target_pairs={{1,0},{2,1},{3,2},{4,3},{5,4},{6,5},{7,6},{0,7},{9,8},{10,9},{11,1... | collective-permute-start | bytes 393224 | tf_op jit(solution)/shard_map/ppermute | solution.py:20
  194.6 7.5 %collective-permute-start.7 = (f32[8,1,32,128]{3,2,1,0:T(8,128)S(1)}, f32[8,1,32,128]{3,2,1,0:T(8,128)S(1)}, u32[]{:S(2)}, u32[]{:S(2)}) collective-permute-start(f32[8,1,32,128]{3,2,1,0:T(8,128)S(1)} %get-tuple-element.194), channel_id=1, source_target_pairs={{0,1},{1,2},{2,3},{3,4},{4,5},{5,6},{6,7},{7,0},{8,9},{9,10},{10,1... | collective-permute-start | bytes 393224 | tf_op jit(solution)/shard_map/ppermute | solution.py:19
Sparse Core Ops, SparseCore 0:
  12.5 135.0 all-gather.1
  164.5 394.7 reduce-scatter.1
where the time goes:
time: 643 us; the launch traced here: 642 us
  waiting for transfers between devices  467 us (73%)
  blocking collectives  75.3 us (12%)
  starting transfers between devices  46.7 us (7%)
  matrix products  16.3 us (3%)
  between operations  14.5 us (2%)
  local copies, waits for them, and re-layouts  11.9 us (2%)
  other arithmetic  10.5 us (2%)
    reduce_scatter x1, waiting for transfers between devices, per_device(): lax.psum_scatter(jnp.einsum('ijkn,ijkcs->ncs', window, far_back, precisio...  355 us
    all_gather x1, waiting for transfers between devices, per_device(): lax.all_gather(coarse_field, 'wide', axis=0, tiled=True)  94.2 us
    psum x1, blocking collectives, per_device(): owned_sum = lax.psum(owned_sum, 'narrow')  75.3 us
    ppermute x4, starting transfers between devices, extended(): after = lax.ppermute(initial, axis, down)  32.3 us
    ppermute x4, starting transfers between devices, extended(): before = lax.ppermute(last, axis, up)  14.3 us
  transfers between devices with their start and end apart: 10, of which 6 were waited for; matrix products, arithmetic and copies ran while one was open for 3% of the time, Pallas kernels for 0%

commit v1 on v0

v1 whole, which is shorter than its diff:
```python
import functools

import jax
import jax.numpy as jnp
from jax import lax
from jax.experimental import pallas as pl
from jax.experimental.pallas import tpu as pltpu
from jax.sharding import PartitionSpec as P

SHAPE_K = 1.25
EXACT = lax.Precision.HIGHEST
MESH = pl.DeviceIdType.MESH
NT = (((1,), (1,)), ((), ()))
NN = (((1,), (0,)), ((), ()))
TN = (((0,), (0,)), ((), ()))
PLACES = ((-1, -1), (-1, 0), (-1, 1), (0, -1), (0, 1), (1, -1), (1, 0), (1, 1))

SLICES = 8
GROUP = 8


def weibull(field, counts, offset):
    return SHAPE_K * (
        jnp.exp(SHAPE_K * (jnp.log(counts.astype(jnp.float32)) - offset - field)) - 1.0
    )


def two(x):
    high = x.astype(jnp.bfloat16)
    return high, (x - high.astype(jnp.float32)).astype(jnp.bfloat16)


def three(x):
    high = x.astype(jnp.bfloat16)
    rest = x - high.astype(jnp.float32)
    middle = rest.astype(jnp.bfloat16)
    return high, middle, (rest - middle.astype(jnp.float32)).astype(jnp.bfloat16)


def dot(a, b, dims):
    return lax.dot_general(a, b, dims, preferred_element_type=jnp.float32)


def dot_split(x, high, low, dims):
    rows = x.shape[0]
    x_high, x_low = two(x)
    both = dot(jnp.concatenate([x_high, x_low], axis=0), high, dims)
    return both[:rows] + both[rows:] + dot(x_high, low, dims)


def dot_pick(pick, values, dims):
    parts = [dot(pick, part, dims) for part in three(values)]
    return parts[0] + (parts[1] + parts[2])


def kernel(
    wide_count,
    narrow_count,
    field_ref,
    counts_ref,
    offset_ref,
    kriging_ref,
    whiten_ref,
    near_ref,
    list_ref,
    home_ref,
    coarse_ref,
    coarse_counts_ref,
    coarse_offset_ref,
    coarse_whiten_ref,
    fine_out,
    coarse_out,
    weights,
    weights_high,
    weights_low,
    gain_high,
    gain_low,
    padded,
    rim,
    rim_in,
    own_slices,
    slices,
    picks,
    far_send,
    far_recv,
    far,
    back_near,
    resid,
    back_white,
    terms_send,
    terms_recv,
    sums,
    sums_in,
    totals,
    spots,
    weight_sems,
    sems,
):
    rows_here, cols_here, chains, sites = field_ref.shape
    blocks = rows_here * cols_here
    owned = coarse_ref.shape[0]
    near_count, far_count = near_ref.shape[2], list_ref.shape[2]
    reads = blocks * far_count
    coarse_total = owned * wide_count
    piece = chains // SLICES
    tile = owned * piece
    message = reads * piece
    near_sites = near_count * sites

    w = lax.axis_index("wide")
    n = lax.axis_index("narrow")
    half = lax.rem(w // 8, 2)
    mine = lax.rem(n, 4) + 4 * half

    def sem(i):
        return sems.at[i]

    weight_copies = [
        pltpu.make_async_copy(kriging_ref.at[b], weights.at[b], weight_sems.at[b])
        for b in range(blocks)
    ]
    for copy in weight_copies:
        copy.start()

    for s in range(SLICES):
        for j in range(owned):
            own_slices[s, j * piece : (j + 1) * piece, :] = coarse_ref[
                j, s * piece : (s + 1) * piece, :
            ]

    lane = lax.broadcasted_iota(jnp.int32, (1, coarse_total), 1)
    for i in range(blocks):
        for j in range(far_count):
            number = list_ref[i // cols_here, i % cols_here, j]
            picks[mine, pl.ds(i * far_count + j, 1), :] = (lane == home_ref[number]).astype(
                jnp.float32
            )

    own_rows = pl.ds(pl.multiple_of(w * tile, tile), tile)
    own_copy = pltpu.make_async_copy(own_slices.at[mine], slices.at[own_rows], sem(1))
    own_copy.start()

    def send_slice(t, carry):
        to = lax.rem(w + t, wide_count)
        part = lax.rem(n, 4) + 4 * lax.rem(to // 8, 2)
        pltpu.make_async_remote_copy(
            src_ref=own_slices.at[part],
            dst_ref=slices.at[own_rows],
            send_sem=sem(0),
            recv_sem=sem(1),
            device_id=(to, n),
            device_id_type=MESH,
        ).start()
        return carry

    lax.fori_loop(1, wide_count, send_slice, 0)

    core, pair, quad = lax.rem(n, 2), lax.rem(n // 2, 2), n // 4
    members = []
    for t in range(1, GROUP):
        c = 1 - core if t % 2 else core
        p = 1 - pair if (t // 2) % 2 else pair
        h = 1 - half if t // 4 else half
        members.append((w + 8 * (h - half), quad * 4 + p * 2 + c, c + 2 * p + 4 * h))

    for to_w, to_n, _ in members:
        pltpu.make_async_remote_copy(
            src_ref=picks.at[mine],
            dst_ref=picks.at[mine],
            send_sem=sem(2),
            recv_sem=sem(3),
            device_id=(to_w, to_n),
            device_id_type=MESH,
        ).start()

    up, down = lax.rem(w + 1, wide_count), lax.rem(w + wide_count - 1, wide_count)
    right, left = lax.rem(n + 1, narrow_count), lax.rem(n + narrow_count - 1, narrow_count)
    last_r, last_c = rows_here, cols_here
    row_spans = {-1: (pl.ds(1, 1), down), 0: (pl.ds(1, rows_here), w), 1: (pl.ds(last_r, 1), up)}
    col_spans = {-1: (pl.ds(1, 1), left), 0: (pl.ds(1, cols_here), n), 1: (pl.ds(last_c, 1), right)}
    rim_rows = {-1: pl.ds(0, 1), 0: pl.ds(1, rows_here), 1: pl.ds(last_r + 1, 1)}
    rim_cols = {-1: pl.ds(0, 1), 0: pl.ds(1, cols_here), 1: pl.ds(last_c + 1, 1)}
    for r in range(rows_here):
        for c in range(cols_here):
            padded[r + 1, c + 1] = field_ref[r, c]
    for dr, dc in PLACES:
        (from_r, to_w), (from_c, to_n) = row_spans[dr], col_spans[dc]
        pltpu.make_async_remote_copy(
            src_ref=padded.at[from_r, from_c],
            dst_ref=padded.at[rim_rows[-dr], rim_cols[-dc]],
            send_sem=sem(4),
            recv_sem=sem(5),
            device_id=(to_w, to_n),
            device_id_type=MESH,
        ).start()

    for b in range(blocks):
        r, c = b // cols_here, b % cols_here
        for k in range(near_count):
            number = near_ref[r, c, k]
            grid_cols = cols_here * narrow_count
            row = number // grid_cols - w * rows_here + 1
            row = jnp.where(row < 0, row + rows_here * wide_count, row)
            row = jnp.where(row > rows_here + 1, row - rows_here * wide_count, row)
            col = lax.rem(number, grid_cols) - n * cols_here + 1
            col = jnp.where(col < 0, col + grid_cols, col)
            col = jnp.where(col > cols_here + 1, col - grid_cols, col)
            row, col = jnp.clip(row, 0, rows_here + 1), jnp.clip(col, 0, cols_here + 1)
            spots[b * near_count + k] = row * (cols_here + 2) + col

    for b in range(blocks):
        gain = lax.dot_general(
            whiten_ref[b], whiten_ref[b], TN, precision=EXACT, preferred_element_type=jnp.float32
        )
        gain_high[b], gain_low[b] = two(gain)
    for j in range(owned):
        white = lax.dot_general(
            coarse_ref[j], coarse_whiten_ref[j], NT, precision=EXACT,
            preferred_element_type=jnp.float32,
        )
        prior = lax.dot_general(
            white, coarse_whiten_ref[j], NN, precision=EXACT, preferred_element_type=jnp.float32
        )
        coarse_out[j] = (
            weibull(coarse_ref[j], coarse_counts_ref[j : j + 1, :], coarse_offset_ref[j : j + 1, :])
            - prior
        )
    for b in range(blocks):
        r, c = b // cols_here, b % cols_here
        fine_out[r, c] = weibull(
            field_ref[r, c], counts_ref[b : b + 1, :], offset_ref[b : b + 1, :]
        )
        weight_copies[b].wait()
        weights_high[b], weights_low[b] = two(weights[b])
        back_near[b, near_count] = jnp.zeros((chains, sites), jnp.float32)

    pltpu.make_async_copy(slices, slices, sem(1)).wait()
    other_picks = picks.at[pl.ds(0, GROUP - 1)]
    pltpu.make_async_copy(other_picks, other_picks, sem(3)).wait()
    held = jnp.concatenate(
        [slices[pl.ds(r, coarse_total, stride=piece), :] for r in range(piece)], axis=1
    )
    pick = jnp.concatenate([picks[s] for s in range(GROUP)], axis=0).astype(jnp.bfloat16)
    chosen = dot_pick(pick, held, NN)
    for r in range(piece):
        far_send[pl.ds(r, GROUP * reads, stride=piece), :] = chosen[:, r * sites : (r + 1) * sites]

    def group_rows(s):
        return pl.ds(pl.multiple_of(s * message, message), message)

    def exchange(source, target, send_sem, recv_sem):
        pltpu.make_async_copy(
            source.at[group_rows(mine)], target.at[group_rows(mine)], recv_sem
        ).start()
        for to_w, to_n, s in members:
            pltpu.make_async_remote_copy(
                src_ref=source.at[group_rows(s)],
                dst_ref=target.at[group_rows(mine)],
                send_sem=send_sem,
                recv_sem=recv_sem,
                device_id=(to_w, to_n),
                device_id_type=MESH,
            ).start()

    exchange(far_send, far_recv, sem(6), sem(7))

    interior = padded.at[pl.ds(0, 4)]
    pltpu.make_async_copy(interior, interior, sem(5)).wait()
    width = cols_here + 2
    for b in range(blocks):
        r, c = b // cols_here, b % cols_here
        fields = []
        for k in range(near_count):
            spot = spots[b * near_count + k]
            fields.append(padded[spot // width, lax.rem(spot, width)])
        near = jnp.concatenate(fields, axis=1)
        resid[b] = field_ref[r, c] - dot_split(
            near, weights_high[b, :, :near_sites], weights_low[b, :, :near_sites], NT
        )

    pltpu.make_async_copy(far_recv, far_recv, sem(7)).wait()
    for s in range(SLICES):
        for i in range(reads):
            far[i, s * piece : (s + 1) * piece, :] = far_recv[
                s * message + i * piece : s * message + (i + 1) * piece, :
            ]
    for b in range(blocks):
        distant = jnp.concatenate([far[b * far_count + j] for j in range(far_count)], axis=1)
        left_over = resid[b] - dot_split(
            distant, weights_high[b, :, near_sites:], weights_low[b, :, near_sites:], NT
        )
        back_white[b] = dot_split(left_over, gain_high[b], gain_low[b], NN)
    for b in range(blocks):
        back = dot_split(
            back_white[b], weights_high[b, :, near_sites:], weights_low[b, :, near_sites:], NN
        )
        for j in range(far_count):
            i = b * far_count + j
            for s in range(SLICES):
                terms_send[s * message + i * piece : s * message + (i + 1) * piece, :] = back[
                    s * piece : (s + 1) * piece, j * sites : (j + 1) * sites
                ]
    exchange(terms_send, terms_recv, sem(8), sem(9))

    for b in range(blocks):
        back = dot_split(
            back_white[b], weights_high[b, :, :near_sites], weights_low[b, :, :near_sites], NN
        )
        for k in range(near_count):
            back_near[b, k] = back[:, k * sites : (k + 1) * sites]
    for pr in range(rows_here + 2):
        for pc in range(cols_here + 2):
            total = None
            for b in range(blocks):
                r, c = b // cols_here + 1, b % cols_here + 1
                if max(abs(r - pr), abs(c - pc)) != 1:
                    continue
                slot = jnp.int32(near_count)
                for k in range(near_count):
                    slot = jnp.where(
                        spots[b * near_count + k] == pr * width + pc, jnp.int32(k), slot
                    )
                term = back_near[b, slot]
                total = term if total is None else total + term
            rim[pr, pc] = total
    for dr, dc in PLACES:
        to_w, to_n = row_spans[dr][1], col_spans[dc][1]
        pltpu.make_async_remote_copy(
            src_ref=rim.at[rim_rows[dr], rim_cols[dc]],
            dst_ref=rim_in.at[rim_rows[-dr], rim_cols[-dc]],
            send_sem=sem(10),
            recv_sem=sem(11),
            device_id=(to_w, to_n),
            device_id_type=MESH,
        ).start()

    pltpu.make_async_copy(terms_recv, terms_recv, sem(9)).wait()
    gathered = jnp.concatenate(
        [terms_recv[pl.ds(r, GROUP * reads, stride=piece), :] for r in range(piece)], axis=1
    )
    summed = dot_pick(pick, gathered, TN)
    for r in range(piece):
        sums[pl.ds(r, coarse_total, stride=piece), :] = summed[:, r * sites : (r + 1) * sites]
    place = (w // 16 * 8 + lax.rem(w, 8)) * 2 + quad

    def send_sum(to):
        rows = pl.ds(pl.multiple_of(to * tile, tile), tile)
        return pltpu.make_async_remote_copy(
            src_ref=sums.at[rows],
            dst_ref=sums_in.at[place],
            send_sem=sem(12),
            recv_sem=sem(13),
            device_id=(to, mine),
            device_id_type=MESH,
        )

    def send_sums(t, carry):
        send_sum(lax.rem(w + t, wide_count)).start()
        return carry

    lax.fori_loop(1, wide_count, send_sums, 0)

    @pl.when(mine == n)
    def _():
        pltpu.make_async_copy(sums.at[own_rows], sums_in.at[place], sem(13)).start()

    @pl.when(mine != n)
    def _():
        send_sum(w).start()

    around = rim_in.at[pl.ds(0, 4)]
    pltpu.make_async_copy(around, around, sem(11)).wait()
    for r in range(rows_here):
        for c in range(cols_here):
            total = fine_out[r, c] - back_white[r * cols_here + c] + rim[r + 1, c + 1]
            edge_r = [e for e, at in ((0, 0), (last_r + 1, rows_here - 1)) if r == at]
            edge_c = [e for e, at in ((0, 0), (last_c + 1, cols_here - 1)) if c == at]
            for e in edge_r:
                total = total + rim_in[e, c + 1]
            for f in edge_c:
                total = total + rim_in[r + 1, f]
            for e in edge_r:
                for f in edge_c:
                    total = total + rim_in[e, f]
            fine_out[r, c] = total

    pltpu.make_async_copy(sums_in, sums_in, sem(13)).wait()
    totals[n] = jnp.sum(sums_in[...], axis=0)
    for t in range(1, narrow_count):
        pltpu.make_async_remote_copy(
            src_ref=totals.at[n],
            dst_ref=totals.at[n],
            send_sem=sem(14),
            recv_sem=sem(15),
            device_id=(w, lax.rem(n + t, narrow_count)),
            device_id_type=MESH,
        ).start()
    other_totals = totals.at[pl.ds(0, narrow_count - 1)]
    pltpu.make_async_copy(other_totals, other_totals, sem(15)).wait()
    for s in range(SLICES):
        for j in range(owned):
            rows = slice(s * piece, (s + 1) * piece)
            coarse_out[j, rows, :] = (
                coarse_out[j, rows, :] + totals[s, j * piece : (j + 1) * piece, :]
            )

    sent = slices.at[pl.ds(0, (wide_count - 1) * tile)]
    pltpu.make_async_copy(sent, sent, sem(0)).wait()
    pltpu.make_async_copy(other_picks, other_picks, sem(2)).wait()
    pltpu.make_async_copy(interior, interior, sem(4)).wait()
    others = far_send.at[pl.ds(0, (GROUP - 1) * message)]
    pltpu.make_async_copy(others, others, sem(6)).wait()
    pltpu.make_async_copy(others, others, sem(8)).wait()
    pltpu.make_async_copy(around, around, sem(10)).wait()
    pltpu.make_async_copy(sent, sent, sem(12)).wait()

    @pl.when(mine != n)
    def _():
        one = sums.at[pl.ds(0, tile)]
        pltpu.make_async_copy(one, one, sem(12)).wait()

    pltpu.make_async_copy(other_totals, other_totals, sem(14)).wait()


def per_device(
    wide_count,
    narrow_count,
    fine_field,
    fine_counts,
    fine_offset,
    kriging,
    whiten,
    neighbours,
    coarse_list,
    coarse_field,
    coarse_counts,
    coarse_offset,
    coarse_whiten,
    coarse_home,
):
    rows_here, cols_here, chains, sites = fine_field.shape
    blocks = rows_here * cols_here
    owned = coarse_field.shape[0]
    cond = kriging.shape[3]
    near_count, far_count = neighbours.shape[2], coarse_list.shape[2]
    reads = blocks * far_count
    piece = chains // SLICES
    f32, bf16 = jnp.float32, jnp.bfloat16
    vmem = pl.BlockSpec(memory_space=pltpu.VMEM)
    smem = pl.BlockSpec(memory_space=pltpu.SMEM)
    return pl.pallas_call(
        functools.partial(kernel, wide_count, narrow_count),
        out_shape=(
            jax.ShapeDtypeStruct(fine_field.shape, f32),
            jax.ShapeDtypeStruct(coarse_field.shape, f32),
        ),
        in_specs=[vmem, vmem, vmem, pl.BlockSpec(memory_space=pl.ANY), vmem, smem, smem, smem]
        + [vmem] * 4,
        out_specs=(vmem, vmem),
        scratch_shapes=[
            pltpu.VMEM((blocks, sites, cond), f32),
            pltpu.VMEM((blocks, sites, cond), bf16),
            pltpu.VMEM((blocks, sites, cond), bf16),
            pltpu.VMEM((blocks, sites, sites), bf16),
            pltpu.VMEM((blocks, sites, sites), bf16),
            pltpu.VMEM((rows_here + 2, cols_here + 2, chains, sites), f32),
            pltpu.VMEM((rows_here + 2, cols_here + 2, chains, sites), f32),
            pltpu.VMEM((rows_here + 2, cols_here + 2, chains, sites), f32),
            pltpu.VMEM((SLICES, owned * piece, sites), f32),
            pltpu.VMEM((wide_count * owned * piece, sites), f32),
            pltpu.VMEM((GROUP, reads, wide_count * owned), f32),
            pltpu.VMEM((GROUP * reads * piece, sites), f32),
            pltpu.VMEM((GROUP * reads * piece, sites), f32),
            pltpu.VMEM((reads, chains, sites), f32),
            pltpu.VMEM((blocks, near_count + 1, chains, sites), f32),
            pltpu.VMEM((blocks, chains, sites), f32),
            pltpu.VMEM((blocks, chains, sites), f32),
            pltpu.VMEM((GROUP * reads * piece, sites), f32),
            pltpu.VMEM((GROUP * reads * piece, sites), f32),
            pltpu.VMEM((wide_count * owned * piece, sites), f32),
            pltpu.VMEM((wide_count, owned * piece, sites), f32),
            pltpu.VMEM((narrow_count, owned * piece, sites), f32),
            pltpu.SMEM((blocks * near_count,), jnp.int32),
            pltpu.SemaphoreType.DMA((blocks,)),
            pltpu.SemaphoreType.DMA((16,)),
        ],
        compiler_params=pltpu.CompilerParams(
            has_side_effects=True, vmem_limit_bytes=60 * 1024 * 1024
        ),
    )(
        fine_field,
        fine_counts.reshape(blocks, sites),
        fine_offset.reshape(blocks, sites),
        kriging.reshape(blocks, sites, cond),
        whiten.reshape(blocks, sites, sites),
        neighbours,
        coarse_list,
        coarse_home,
        coarse_field,
        coarse_counts,
        coarse_offset,
        coarse_whiten,
    )


def solution(mesh):
    return jax.shard_map(
        functools.partial(per_device, mesh.shape["wide"], mesh.shape["narrow"]),
        mesh=mesh,
        in_specs=(
            P("wide", "narrow", None, None),
            P("wide", "narrow", None),
            P("wide", "narrow", None),
            P("wide", "narrow", None, None),
            P("wide", "narrow", None, None),
            P("wide", "narrow", None),
            P("wide", "narrow", None),
            P("wide", None, None),
            P("wide", None),
            P("wide", None),
            P("wide", None, None),
            P(),
        ),
        out_specs=(P("wide", "narrow", None, None), P("wide", None, None)),
        check_vma=False,
    )
```

time: 643 us -> 78.2 us (0.12)
  waiting for transfers between devices: 467 us -> 0 us
  blocking collectives: 75.3 us -> 0 us
  Pallas kernels: 0 us -> 73 us
  starting transfers between devices: 46.7 us -> 0 us
  matrix products: 16.3 us -> 0 us
  between operations: 14.5 us -> 0.64 us
  other arithmetic: 10.5 us -> 0 us
  local copies, waits for them, and re-layouts: 11.9 us -> 4.3 us
    reduce_scatter x1 -> x0, waiting for transfers between devices: 355 us -> none  [per_device(): lax.psum_scatter(jnp.einsum('ijkn,ijkcs->ncs', window, far_back, precisio...]
    all_gather x1 -> x0, waiting for transfers between devices: 94.2 us -> none  [per_device(): lax.all_gather(coarse_field, 'wide', axis=0, tiled=True)]
    psum x1 -> x0, blocking collectives: 75.3 us -> none  [per_device(): owned_sum = lax.psum(owned_sum, 'narrow')]
    pallas_call x0 -> x1, Pallas kernels: none -> 73 us  [per_device(): pl.pallas_call(functools.partial(kernel, wide_count, narrow_count), out_s...]
    ppermute x8 -> x0, starting transfers between devices: 46.7 us -> none  [the longest x4 32.3 us: extended(): after = lax.ppermute(initial, axis, down)]
    ppermute x8 -> x0, waiting for transfers between devices: 17.1 us -> none  [the longest x4 12.2 us: extended(): before = lax.ppermute(last, axis, up)]
    dot_general x10 -> x0, matrix products: 16.3 us -> none  [the longest x1 3.86 us: per_device(): jnp.einsum('ijcs,ijskm->ijkcm', back_white, weights, precision=EXACT)]
  transfers between devices with their start and end apart: 10 -> 0, of which waited for: 6 -> 0; matrix products, arithmetic and copies ran while one was open for 3% -> 0% of each run, Pallas kernels for 0% -> 0%
where the time goes in v1:
time: 78.2 us; the launch traced here: 77.9 us
  Pallas kernels  73 us (93%)
  local copies, waits for them, and re-layouts  4.3 us (5%)
    pallas_call x1, Pallas kernels, per_device(): pl.pallas_call(functools.partial(kernel, wide_count, narrow_count), out_s...  73 us
    unnamed x3, local copies, waits for them, and re-layouts  4.3 us

profile of v1, /device:TPU:1, one launch (start us, length us, event | category | flops | bytes accessed | tf_op | source)
XLA Modules:
  0.0 77.9 jit_solution(15852573087916736472)
XLA Ops:
  0.6 1.4 %copy.14.list_ref = s32[4,2,3]{2,1,0:T(2,128)} copy(s32[4,2,3]{0,1,2:T(2,128)} %param.18) | data formatting | bytes 192 | tf_op args[6]
  2.0 73.0 %shard_map.131 = (f32[4,2,32,128]{3,2,1,0:T(8,128)}, f32[2,32,128]{2,1,0:T(8,128)}) custom-call(f32[4,2,32,128]{3,2,1,0:T(8,128)} %field_ref.1, s32[8,128]{1,0:T(8,128)} %bitcast.6, f32[8,128]{1,0:T(8,128)} %bitcast.7, f32[8,128,896]{2,1,0:T(8,128)} %bitcast.4, f32[8,128,128]{2,1,0:T(8,128)} %bitcast.5, s32[4,2,4]{2,1,0:T(2,128)} %near_ref.1, ...), custom_call_target="tpu_custom_call" | custom-call | tf_op jit(solution)/shard_map/pallas_call | solution.py:451
  75.0 1.6 %copy.17 = f32[4,2,32,128]{3,2,1,0:T(8,128)} copy(f32[4,2,32,128]{3,2,1,0:T(8,128)} %get-tuple-element.4) | data formatting | bytes 262144
  76.5 1.4 %copy.18 = f32[2,32,128]{2,1,0:T(8,128)} copy(f32[2,32,128]{2,1,0:T(8,128)} %get-tuple-element.5) | data formatting | bytes 65536

commit v2 on v1

--- a/solution.py
+++ b/solution.py
@@ -15,6 +15,7 @@
 TN = (((0,), (0,)), ((), ()))
 PLACES = ((-1, -1), (-1, 0), (-1, 1), (0, -1), (0, 1), (1, -1), (1, 0), (1, 1))
 
+RUN = 4
 SLICES = 8
 GROUP = 8
 
@@ -56,50 +57,57 @@
 def kernel(
     wide_count,
     narrow_count,
-    field_ref,
-    counts_ref,
-    offset_ref,
     kriging_ref,
-    whiten_ref,
-    near_ref,
-    list_ref,
-    home_ref,
-    coarse_ref,
-    coarse_counts_ref,
-    coarse_offset_ref,
-    coarse_whiten_ref,
-    fine_out,
-    coarse_out,
-    weights,
-    weights_high,
-    weights_low,
-    gain_high,
-    gain_low,
-    padded,
-    rim,
-    rim_in,
-    own_slices,
-    slices,
-    picks,
-    far_send,
-    far_recv,
-    far,
-    back_near,
-    resid,
-    back_white,
-    terms_send,
-    terms_recv,
-    sums,
-    sums_in,
-    totals,
-    spots,
-    weight_sems,
-    sems,
+    *refs,
 ):
+    inputs, (fine_out, coarse_out), held_here = refs[:11], refs[11:13], refs[13:24]
+    (
+        field_ref,
+        counts_ref,
+        offset_ref,
+        whiten_ref,
+        near_ref,
+        list_ref,
+        home_ref,
+        coarse_ref,
+        coarse_counts_ref,
+        coarse_offset_ref,
+        coarse_whiten_ref,
+    ) = held_here
+    (
+        weights,
+        weights_high,
+        weights_low,
+        gain_high,
+        gain_low,
+        padded,
+        rim,
+        rim_in,
+        own_slices,
+        slices,
+        picks,
+        far_send,
+        far_recv,
+        far,
+        back_near,
+        resid,
+        back_white,
+        terms_send,
+        terms_recv,
+        sums,
+        sums_beside,
+        plane_sums,
+        sums_in,
+        totals,
+        spots,
+        weight_sems,
+        sems,
+        copy_sems,
+    ) = refs[24:]
     rows_here, cols_here, chains, sites = field_ref.shape
     blocks = rows_here * cols_here
     owned = coarse_ref.shape[0]
-    near_count, far_count = near_ref.shape[2], list_ref.shape[2]
+    near_count, far_count = near_ref.shape[2], list_ref.shape[0]
     reads = blocks * far_count
     coarse_total = owned * wide_count
     piece = chains // SLICES
@@ -111,49 +119,23 @@
     n = lax.axis_index("narrow")
     half = lax.rem(w // 8, 2)
     mine = lax.rem(n, 4) + 4 * half
+    planes = wide_count // RUN
+    x, plane = lax.rem(w, RUN), w // RUN
+    place = x * planes + plane
 
     def sem(i):
         return sems.at[i]
 
+    copies = {}
+    for i in (7, 4, 5, 6, 0, 1, 2, 8, 9, 10, 3):
+        copies[i] = pltpu.make_async_copy(inputs[i], held_here[i], copy_sems.at[i])
+        copies[i].start()
     weight_copies = [
         pltpu.make_async_copy(kriging_ref.at[b], weights.at[b], weight_sems.at[b])
         for b in range(blocks)
     ]
     for copy in weight_copies:
         copy.start()
-
-    for s in range(SLICES):
-        for j in range(owned):
-            own_slices[s, j * piece : (j + 1) * piece, :] = coarse_ref[
-                j, s * piece : (s + 1) * piece, :
-            ]
-
-    lane = lax.broadcasted_iota(jnp.int32, (1, coarse_total), 1)
-    for i in range(blocks):
-        for j in range(far_count):
-            number = list_ref[i // cols_here, i % cols_here, j]
-            picks[mine, pl.ds(i * far_count + j, 1), :] = (lane == home_ref[number]).astype(
-                jnp.float32
-            )
-
-    own_rows = pl.ds(pl.multiple_of(w * tile, tile), tile)
-    own_copy = pltpu.make_async_copy(own_slices.at[mine], slices.at[own_rows], sem(1))
-    own_copy.start()
-
-    def send_slice(t, carry):
-        to = lax.rem(w + t, wide_count)
-        part = lax.rem(n, 4) + 4 * lax.rem(to // 8, 2)
-        pltpu.make_async_remote_copy(
-            src_ref=own_slices.at[part],
-            dst_ref=slices.at[own_rows],
-            send_sem=sem(0),
-            recv_sem=sem(1),
-            device_id=(to, n),
-            device_id_type=MESH,
-        ).start()
-        return carry
-
-    lax.fori_loop(1, wide_count, send_slice, 0)
 
     core, pair, quad = lax.rem(n, 2), lax.rem(n // 2, 2), n // 4
     members = []
@@ -162,6 +144,77 @@
         p = 1 - pair if (t // 2) % 2 else pair
         h = 1 - half if t // 4 else half
         members.append((w + 8 * (h - half), quad * 4 + p * 2 + c, c + 2 * p + 4 * h))
+    up, down = lax.rem(w + 1, wide_count), lax.rem(w + wide_count - 1, wide_count)
+    right, left = lax.rem(n + 1, narrow_count), lax.rem(n + narrow_count - 1, narrow_count)
+
+    barrier = pltpu.get_barrier_semaphore()
+
+    def greet(to_w, to_n):
+        pl.semaphore_signal(barrier, inc=1, device_id=(to_w, to_n), device_id_type=MESH)
+
+    def across(t):
+        return lax.rem(plane + t, planes)
+
+    def beside(t):
+        return lax.rem(x + t, RUN)
+
+    def greet_planes(t, carry):
+        greet(across(t) * RUN + x, n)
+        return carry
+
+    lax.fori_loop(1, planes, greet_planes, 0)
+    for t in range(1, RUN):
+        greet(plane * RUN + beside(t), n)
+    for t in range(1, narrow_count):
+        greet(w, lax.rem(n + t, narrow_count))
+    for to_w, to_n, _ in members[4:]:
+        greet(to_w, to_n)
+    for to_w in (up, down):
+        for to_n in (left, n, right):
+            greet(to_w, to_n)
+    greetings = planes - 1 + RUN - 1 + narrow_count - 1 + 3 + 6
+
+    copies[7].wait()
+    for s in range(SLICES):
+        for j in range(owned):
+            own_slices[s, j * piece : (j + 1) * piece, :] = coarse_ref[
+                j, s * piece : (s + 1) * piece, :
+            ]
+
+    copies[5].wait()
+    copies[6].wait()
+    lane = lax.broadcasted_iota(jnp.int32, (1, coarse_total), 1)
+    for i in range(blocks):
+        for j in range(far_count):
+            number = list_ref[j, i % cols_here, i // cols_here]
+            owner, which = home_ref[number] // owned, lax.rem(home_ref[number], owned)
+            column = (lax.rem(owner, RUN) * planes + owner // RUN) * owned + which
+            picks[mine, pl.ds(i * far_count + j, 1), :] = (lane == column).astype(jnp.float32)
+
+    copies[0].wait()
+    for r in range(rows_here):
+        for c in range(cols_here):
+            padded[r + 1, c + 1] = field_ref[r, c]
+
+    pl.semaphore_wait(barrier, greetings)
+    own_rows = pl.ds(pl.multiple_of(place * tile, tile), tile)
+    own_copy = pltpu.make_async_copy(own_slices.at[mine], slices.at[own_rows], sem(1))
+    own_copy.start()
+
+    def send_slice(t, carry):
+        to = across(t) * RUN + x
+        part = lax.rem(n, 4) + 4 * lax.rem(to // 8, 2)
+        pltpu.make_async_remote_copy(
+            src_ref=own_slices.at[part],
+            dst_ref=slices.at[own_rows],
+            send_sem=sem(0),
+            recv_sem=sem(1),
+            device_id=(to, n),
+            device_id_type=MESH,
+        ).start()
+        return carry
+
+    lax.fori_loop(1, planes, send_slice, 0)
 
     for to_w, to_n, _ in members:
         pltpu.make_async_remote_copy(
@@ -173,16 +226,11 @@
             device_id_type=MESH,
         ).start()
 
-    up, down = lax.rem(w + 1, wide_count), lax.rem(w + wide_count - 1, wide_count)
-    right, left = lax.rem(n + 1, narrow_count), lax.rem(n + narrow_count - 1, narrow_count)
     last_r, last_c = rows_here, cols_here
     row_spans = {-1: (pl.ds(1, 1), down), 0: (pl.ds(1, rows_here), w), 1: (pl.ds(last_r, 1), up)}
     col_spans = {-1: (pl.ds(1, 1), left), 0: (pl.ds(1, cols_here), n), 1: (pl.ds(last_c, 1), right)}
     rim_rows = {-1: pl.ds(0, 1), 0: pl.ds(1, rows_here), 1: pl.ds(last_r + 1, 1)}
     rim_cols = {-1: pl.ds(0, 1), 0: pl.ds(1, cols_here), 1: pl.ds(last_c + 1, 1)}
-    for r in range(rows_here):
-        for c in range(cols_here):
-            padded[r + 1, c + 1] = field_ref[r, c]
     for dr, dc in PLACES:
         (from_r, to_w), (from_c, to_n) = row_spans[dr], col_spans[dc]
         pltpu.make_async_remote_copy(
@@ -194,6 +242,23 @@
             device_id_type=MESH,
         ).start()
 
+    def run_rows(at):
+        return pl.ds(pl.multiple_of(at * planes * tile, planes * tile), planes * tile)
+
+    gathered_here = slices.at[run_rows(x)]
+    pltpu.make_async_copy(gathered_here, gathered_here, sem(1)).wait()
+    for t in range(1, RUN):
+        pltpu.make_async_remote_copy(
+            src_ref=gathered_here,
+            dst_ref=gathered_here,
+            send_sem=sem(16),
+            recv_sem=sem(17),
+            device_id=(plane * RUN + beside(t), n),
+            device_id_type=MESH,
+        ).start()
+    other_runs = slices.at[pl.ds(0, (RUN - 1) * planes * tile)]
+
+    copies[4].wait()
     for b in range(blocks):
         r, c = b // cols_here, b % cols_here
         for k in range(near_count):
@@ -208,6 +273,8 @@
             row, col = jnp.clip(row, 0, rows_here + 1), jnp.clip(col, 0, cols_here + 1)
             spots[b * near_count + k] = row * (cols_here + 2) + col
 
+    for i in (1, 2, 3, 8, 9, 10):
+        copies[i].wait()
     for b in range(blocks):
         gain = lax.dot_general(
             whiten_ref[b], whiten_ref[b], TN, precision=EXACT, preferred_element_type=jnp.float32
@@ -234,7 +301,7 @@
         weights_high[b], weights_low[b] = two(weights[b])
         back_near[b, near_count] = jnp.zeros((chains, sites), jnp.float32)
 
-    pltpu.make_async_copy(slices, slices, sem(1)).wait()
+    pltpu.make_async_copy(other_runs, other_runs, sem(17)).wait()
     other_picks = picks.at[pl.ds(0, GROUP - 1)]
     pltpu.make_async_copy(other_picks, other_picks, sem(3)).wait()
     held = jnp.concatenate(
@@ -341,32 +408,33 @@
     summed = dot_pick(pick, gathered, TN)
     for r in range(piece):
         sums[pl.ds(r, coarse_total, stride=piece), :] = summed[:, r * sites : (r + 1) * sites]
-    place = (w // 16 * 8 + lax.rem(w, 8)) * 2 + quad
-
-    def send_sum(to):
-        rows = pl.ds(pl.multiple_of(to * tile, tile), tile)
-        return pltpu.make_async_remote_copy(
-            src_ref=sums.at[rows],
-            dst_ref=sums_in.at[place],
+
+    pltpu.make_async_copy(sums.at[run_rows(x)], sums_beside.at[x], sem(19)).start()
+    for t in range(1, RUN):
+        pltpu.make_async_remote_copy(
+            src_ref=sums.at[run_rows(beside(t))],
+            dst_ref=sums_beside.at[x],
+            send_sem=sem(18),
+            recv_sem=sem(19),
+            device_id=(plane * RUN + beside(t), n),
+            device_id_type=MESH,
+        ).start()
+    pltpu.make_async_copy(sums_beside, sums_beside, sem(19)).wait()
+    plane_sums[...] = jnp.sum(sums_beside[...], axis=0).reshape(planes, tile, sites)
+    pltpu.make_async_copy(plane_sums.at[plane], sums_in.at[plane], sem(13)).start()
+
+    def send_sums(t, carry):
+        pltpu.make_async_remote_copy(
+            src_ref=plane_sums.at[across(t)],
+            dst_ref=sums_in.at[plane],
             send_sem=sem(12),
             recv_sem=sem(13),
-            device_id=(to, mine),
-            device_id_type=MESH,
-        )
-
-    def send_sums(t, carry):
-        send_sum(lax.rem(w + t, wide_count)).start()
+            device_id=(across(t) * RUN + x, n),
+            device_id_type=MESH,
+        ).start()
         return carry
 
-    lax.fori_loop(1, wide_count, send_sums, 0)
-
-    @pl.when(mine == n)
-    def _():
-        pltpu.make_async_copy(sums.at[own_rows], sums_in.at[place], sem(13)).start()
-
-    @pl.when(mine != n)
-    def _():
-        send_sum(w).start()
+    lax.fori_loop(1, planes, send_sums, 0)
 
     around = rim_in.at[pl.ds(0, 4)]
     pltpu.make_async_copy(around, around, sem(11)).wait()
@@ -385,7 +453,9 @@
             fine_out[r, c] = total
 
     pltpu.make_async_copy(sums_in, sums_in, sem(13)).wait()
-    totals[n] = jnp.sum(sums_in[...], axis=0)
+    totals[n] = jnp.sum(
+        sums_in[...].reshape(planes // 4, 2, 2, tile, sites), axis=(0, 2)
+    )
     for t in range(1, narrow_count):
         pltpu.make_async_remote_copy(
             src_ref=totals.at[n],
@@ -401,11 +471,15 @@
         for j in range(owned):
             rows = slice(s * piece, (s + 1) * piece)
             coarse_out[j, rows, :] = (
-                coarse_out[j, rows, :] + totals[s, j * piece : (j + 1) * piece, :]
+                coarse_out[j, rows, :]
+                + totals[s % 4, s // 4, j * piece : (j + 1) * piece, :]
+                + totals[s % 4 + 4, s // 4, j * piece : (j + 1) * piece, :]
             )
 
-    sent = slices.at[pl.ds(0, (wide_count - 1) * tile)]
+    sent = sums_in.at[pl.ds(0, planes - 1)]
     pltpu.make_async_copy(sent, sent, sem(0)).wait()
+    pltpu.make_async_copy(other_runs, other_runs, sem(16)).wait()
+    pltpu.make_async_copy(other_runs, other_runs, sem(18)).wait()
     pltpu.make_async_copy(other_picks, other_picks, sem(2)).wait()
     pltpu.make_async_copy(interior, interior, sem(4)).wait()
     others = far_send.at[pl.ds(0, (GROUP - 1) * message)]
@@ -413,11 +487,6 @@
     pltpu.make_async_copy(others, others, sem(8)).wait()
     pltpu.make_async_copy(around, around, sem(10)).wait()
     pltpu.make_async_copy(sent, sent, sem(12)).wait()
-
-    @pl.when(mine != n)
-    def _():
-        one = sums.at[pl.ds(0, tile)]
-        pltpu.make_async_copy(one, one, sem(12)).wait()
 
     pltpu.make_async_copy(other_totals, other_totals, sem(14)).wait()
 
@@ -447,17 +516,32 @@
     piece = chains // SLICES
     f32, bf16 = jnp.float32, jnp.bfloat16
     vmem = pl.BlockSpec(memory_space=pltpu.VMEM)
-    smem = pl.BlockSpec(memory_space=pltpu.SMEM)
+    operands = (
+        fine_field,
+        fine_counts.reshape(blocks, sites),
+        fine_offset.reshape(blocks, sites),
+        whiten.reshape(blocks, sites, sites),
+        neighbours,
+        coarse_list.transpose(2, 1, 0),
+        coarse_home,
+        coarse_field,
+        coarse_counts,
+        coarse_offset,
+        coarse_whiten,
+    )
     return pl.pallas_call(
         functools.partial(kernel, wide_count, narrow_count),
         out_shape=(
-            jax.ShapeDtypeStruct(fine_field.shape, f32),
-            jax.ShapeDtypeStruct(coarse_field.shape, f32),
+            pltpu.VMEM(fine_field.shape, f32),
+            pltpu.VMEM(coarse_field.shape, f32),
         ),
-        in_specs=[vmem, vmem, vmem, pl.BlockSpec(memory_space=pl.ANY), vmem, smem, smem, smem]
-        + [vmem] * 4,
+        in_specs=[pl.BlockSpec(memory_space=pltpu.HBM)] * (1 + len(operands)),
         out_specs=(vmem, vmem),
         scratch_shapes=[
+            (pltpu.SMEM if i in (4, 5, 6) else pltpu.VMEM)(x.shape, x.dtype)
+            for i, x in enumerate(operands)
+        ]
+        + [
             pltpu.VMEM((blocks, sites, cond), f32),
             pltpu.VMEM((blocks, sites, cond), bf16),
             pltpu.VMEM((blocks, sites, cond), bf16),
@@ -478,29 +562,19 @@
             pltpu.VMEM((GROUP * reads * piece, sites), f32),
             pltpu.VMEM((GROUP * reads * piece, sites), f32),
             pltpu.VMEM((wide_count * owned * piece, sites), f32),
-            pltpu.VMEM((wide_count, owned * piece, sites), f32),
-            pltpu.VMEM((narrow_count, owned * piece, sites), f32),
+            pltpu.VMEM((RUN, wide_count // RUN * owned * piece, sites), f32),
+            pltpu.VMEM((wide_count // RUN, owned * piece, sites), f32),
+            pltpu.VMEM((wide_count // RUN, owned * piece, sites), f32),
+            pltpu.VMEM((narrow_count, 2, owned * piece, sites), f32),
             pltpu.SMEM((blocks * near_count,), jnp.int32),
             pltpu.SemaphoreType.DMA((blocks,)),
-            pltpu.SemaphoreType.DMA((16,)),
+            pltpu.SemaphoreType.DMA((20,)),
+            pltpu.SemaphoreType.DMA((len(operands),)),
         ],
         compiler_params=pltpu.CompilerParams(
-            has_side_effects=True, vmem_limit_bytes=60 * 1024 * 1024
+            collective_id=0, has_side_effects=True, vmem_limit_bytes=60 * 1024 * 1024
         ),
-    )(
-        fine_field,
-        fine_counts.reshape(blocks, sites),
-        fine_offset.reshape(blocks, sites),
-        kriging.reshape(blocks, sites, cond),
-        whiten.reshape(blocks, sites, sites),
-        neighbours,
-        coarse_list,
-        coarse_home,
-        coarse_field,
-        coarse_counts,
-        coarse_offset,
-        coarse_whiten,
-    )
+    )(kriging.reshape(blocks, sites, cond), *operands)
 
 
 def solution(mesh):

time: 78.2 us -> 63.9 us (0.82)
  Pallas kernels: 73 us -> 61.8 us
  local copies, waits for them, and re-layouts: 4.3 us -> 1.27 us
    pallas_call x1, Pallas kernels: 73 us -> 61.8 us  [per_device(): pl.pallas_call(functools.partial(kernel, wide_count, narrow_count), out_s...]
    unnamed x3 -> x2, local copies, waits for them, and re-layouts: 4.3 us -> 1.27 us
where the time goes in v2:
time: 63.9 us; the launch traced here: 63.8 us
  Pallas kernels  61.8 us (97%)
  local copies, waits for them, and re-layouts  1.27 us (2%)
  between operations  0.64 us (1%)
    pallas_call x1, Pallas kernels, per_device(): pl.pallas_call(functools.partial(kernel, wide_count, narrow_count), out_s...  61.8 us

profile of v2, /device:TPU:1, one launch (start us, length us, event | category | flops | bytes accessed | tf_op | source)
XLA Modules:
  0.0 63.8 jit_solution(7748541595916979558)
XLA Ops:
  0.6 61.8 %shard_map.131 = (f32[4,2,32,128]{3,2,1,0:T(8,128)S(1)}, f32[2,32,128]{2,1,0:T(8,128)S(1)}) custom-call(f32[8,128,896]{2,1,0:T(8,128)} %bitcast.5, f32[4,2,32,128]{3,2,1,0:T(8,128)} %refs_0_.1, s32[8,128]{1,0:T(8,128)} %bitcast.7, f32[8,128]{1,0:T(8,128)} %bitcast.8, f32[8,128,128]{2,1,0:T(8,128)} %bitcast.6, s32[4,2,4]{2,1,0:T(2,128)} %refs_4_.1, ...), custom_call_target="tpu_custom_call" | custom-call | tf_op jit(solution)/shard_map/pallas_call | solution.py:532
  62.5 0.7 %copy.16 = f32[4,2,32,128]{3,2,1,0:T(8,128)} copy(f32[4,2,32,128]{3,2,1,0:T(8,128)S(1)} %get-tuple-element.2) | data formatting | bytes 262144
  63.1 0.6 copy.17

commit v3 on v2

--- a/solution.py
+++ b/solution.py
@@ -13,11 +13,23 @@
 NT = (((1,), (1,)), ((), ()))
 NN = (((1,), (0,)), ((), ()))
 TN = (((0,), (0,)), ((), ()))
-PLACES = ((-1, -1), (-1, 0), (-1, 1), (0, -1), (0, 1), (1, -1), (1, 0), (1, 1))
 
 RUN = 4
 SLICES = 8
-GROUP = 8
+PARTS = 4
+
+AROUND = [(dy, dz, dc) for dy in (0, 1, -1) for dz in (0, 1, -1) for dc in (0, 1)]
+
+
+def taken(dy, dz):
+    if dy and dz:
+        return (0 if dy > 0 else 2) + (0 if dz > 0 else 1), 1
+    if dy or dz:
+        return (0 if dy + dz > 0 else 2), 2
+    return 0, PARTS
+
+
+STARTS = [sum(taken(-dy, -dz)[1] for dy, dz, _ in AROUND[:e]) for e in range(len(AROUND))]
 
 
 def weibull(field, counts, offset):
@@ -86,6 +98,7 @@
         own_slices,
         slices,
         picks,
+        all_picks,
         far_send,
         far_recv,
         far,
@@ -111,6 +124,7 @@
     reads = blocks * far_count
     coarse_total = owned * wide_count
     piece = chains // SLICES
+    quarter = reads // PARTS
     tile = owned * piece
     message = reads * piece
     near_sites = near_count * sites
@@ -125,6 +139,52 @@
 
     def sem(i):
         return sems.at[i]
+
+    core, high = lax.rem(n, 2), lax.rem(plane, 2)
+    depth = planes // 2
+    y, z = high * 4 + n // 2, plane // 2
+    members = []
+    for dy, dz, dc in AROUND:
+        to_y, to_z = lax.rem(y + dy + 8, 8), lax.rem(z + dz + depth, depth)
+        to_core = 1 - core if dc else core
+        members.append(
+            (
+                (to_z * 2 + to_y // 4) * RUN + x,
+                lax.rem(to_y, 4) * 2 + to_core,
+                to_core + 2 * lax.rem(to_y, 2) + 4 * lax.rem(to_z, 2),
+            )
+        )
+    up, down = lax.rem(w + 1, wide_count), lax.rem(w + wide_count - 1, wide_count)
+    right, left = lax.rem(n + 1, narrow_count), lax.rem(n + narrow_count - 1, narrow_count)
+
+    barrier = pltpu.get_barrier_semaphore()
+
+    def greet(to_w, to_n):
+        pl.semaphore_signal(barrier, inc=1, device_id=(to_w, to_n), device_id_type=MESH)
+
+    def across(t):
+        return lax.rem(plane + t, planes)
+
+    def beside(t):
+        return lax.rem(x + t, RUN)
+
+    def column(to):
+        return lax.rem(n + (narrow_count // 2) * lax.rem(to + plane, 2), narrow_count)
+
+    def greet_planes(t, carry):
+        greet(across(t) * RUN + x, column(across(t)))
+        return carry
+
+    lax.fori_loop(1, planes, greet_planes, 0)
+    for t in range(1, RUN):
+        greet(plane * RUN + beside(t), n)
+    for t in range(1, narrow_count):
+        greet(w, lax.rem(n + t, narrow_count))
+    for to_w, to_n, _ in members[1:]:
+        greet(to_w, to_n)
+    greet(up, n)
+    greet(down, n)
+    greetings = planes - 1 + RUN - 1 + narrow_count - 1 + len(AROUND) - 1 + 2
 
     copies = {}
     for i in (7, 4, 5, 6, 0, 1, 2, 8, 9, 10, 3):
@@ -137,64 +197,12 @@
     for copy in weight_copies:
         copy.start()
 
-    core, pair, quad = lax.rem(n, 2), lax.rem(n // 2, 2), n // 4
-    members = []
-    for t in range(1, GROUP):
-        c = 1 - core if t % 2 else core
-        p = 1 - pair if (t // 2) % 2 else pair
-        h = 1 - half if t // 4 else half
-        members.append((w + 8 * (h - half), quad * 4 + p * 2 + c, c + 2 * p + 4 * h))
-    up, down = lax.rem(w + 1, wide_count), lax.rem(w + wide_count - 1, wide_count)
-    right, left = lax.rem(n + 1, narrow_count), lax.rem(n + narrow_count - 1, narrow_count)
-
-    barrier = pltpu.get_barrier_semaphore()
-
-    def greet(to_w, to_n):
-        pl.semaphore_signal(barrier, inc=1, device_id=(to_w, to_n), device_id_type=MESH)
-
-    def across(t):
-        return lax.rem(plane + t, planes)
-
-    def beside(t):
-        return lax.rem(x + t, RUN)
-
-    def greet_planes(t, carry):
-        greet(across(t) * RUN + x, n)
-        return carry
-
-    lax.fori_loop(1, planes, greet_planes, 0)
-    for t in range(1, RUN):
-        greet(plane * RUN + beside(t), n)
-    for t in range(1, narrow_count):
-        greet(w, lax.rem(n + t, narrow_count))
-    for to_w, to_n, _ in members[4:]:
-        greet(to_w, to_n)
-    for to_w in (up, down):
-        for to_n in (left, n, right):
-            greet(to_w, to_n)
-    greetings = planes - 1 + RUN - 1 + narrow_count - 1 + 3 + 6
-
     copies[7].wait()
     for s in range(SLICES):
         for j in range(owned):
             own_slices[s, j * piece : (j + 1) * piece, :] = coarse_ref[
                 j, s * piece : (s + 1) * piece, :
             ]
-
-    copies[5].wait()
-    copies[6].wait()
-    lane = lax.broadcasted_iota(jnp.int32, (1, coarse_total), 1)
-    for i in range(blocks):
-        for j in range(far_count):
-            number = list_ref[j, i % cols_here, i // cols_here]
-            owner, which = home_ref[number] // owned, lax.rem(home_ref[number], owned)
-            column = (lax.rem(owner, RUN) * planes + owner // RUN) * owned + which
-            picks[mine, pl.ds(i * far_count + j, 1), :] = (lane == column).astype(jnp.float32)
-
-    copies[0].wait()
-    for r in range(rows_here):
-        for c in range(cols_here):
-            padded[r + 1, c + 1] = field_ref[r, c]
 
     pl.semaphore_wait(barrier, greetings)
     own_rows = pl.ds(pl.multiple_of(place * tile, tile), tile)
@@ -209,38 +217,59 @@
             dst_ref=slices.at[own_rows],
             send_sem=sem(0),
             recv_sem=sem(1),
-            device_id=(to, n),
+            device_id=(to, column(across(t))),
             device_id_type=MESH,
         ).start()
         return carry
 
     lax.fori_loop(1, planes, send_slice, 0)
 
-    for to_w, to_n, _ in members:
+    copies[0].wait()
+
+    def send(source, target, i, to_w, to_n):
         pltpu.make_async_remote_copy(
-            src_ref=picks.at[mine],
-            dst_ref=picks.at[mine],
-            send_sem=sem(2),
-            recv_sem=sem(3),
+            src_ref=source,
+            dst_ref=target,
+            send_sem=sem(i),
+            recv_sem=sem(i + 1),
             device_id=(to_w, to_n),
             device_id_type=MESH,
         ).start()
 
-    last_r, last_c = rows_here, cols_here
-    row_spans = {-1: (pl.ds(1, 1), down), 0: (pl.ds(1, rows_here), w), 1: (pl.ds(last_r, 1), up)}
-    col_spans = {-1: (pl.ds(1, 1), left), 0: (pl.ds(1, cols_here), n), 1: (pl.ds(last_c, 1), right)}
-    rim_rows = {-1: pl.ds(0, 1), 0: pl.ds(1, rows_here), 1: pl.ds(last_r + 1, 1)}
-    rim_cols = {-1: pl.ds(0, 1), 0: pl.ds(1, cols_here), 1: pl.ds(last_c + 1, 1)}
-    for dr, dc in PLACES:
-        (from_r, to_w), (from_c, to_n) = row_spans[dr], col_spans[dc]
-        pltpu.make_async_remote_copy(
-            src_ref=padded.at[from_r, from_c],
-            dst_ref=padded.at[rim_rows[-dr], rim_cols[-dc]],
-            send_sem=sem(4),
-            recv_sem=sem(5),
-            device_id=(to_w, to_n),
-            device_id_type=MESH,
-        ).start()
+    def arrived(i, rows):
+        part = padded.at[pl.ds(0, rows)]
+        pltpu.make_async_copy(part, part, sem(i)).wait()
+
+    rows_mid, cols_mid = pl.ds(1, rows_here), pl.ds(1, cols_here)
+    far_r, far_c = rows_here + 1, cols_here + 1
+    send(field_ref.at[rows_here - 1], padded.at[0, cols_mid], 4, up, n)
+    send(field_ref.at[0], padded.at[far_r, cols_mid], 4, down, n)
+    send(field_ref.at[:, cols_here - 1], padded.at[rows_mid, 0], 20, w, right)
+    send(field_ref.at[:, 0], padded.at[rows_mid, far_c], 20, w, left)
+
+    copies[5].wait()
+    copies[6].wait()
+    lane = lax.broadcasted_iota(jnp.int32, (1, coarse_total), 1)
+    for i in range(blocks):
+        for j in range(far_count):
+            number = list_ref[j, i % cols_here, i // cols_here]
+            owner, which = home_ref[number] // owned, lax.rem(home_ref[number], owned)
+            at = (lax.rem(owner, RUN) * planes + owner // RUN) * owned + which
+            q, i_q = divmod(i * far_count + j, quarter)
+            picks[0, q, i_q : i_q + 1, :] = (lane == at).astype(jnp.float32)
+
+    for (dy, dz, dc), (to_w, to_n, _) in zip(AROUND[1:], members[1:]):
+        first, count = taken(dy, dz)
+        send(
+            picks.at[0, pl.ds(first, count)],
+            picks.at[AROUND.index((-dy, -dz, dc)), pl.ds(first, count)],
+            2,
+            to_w,
+            to_n,
+        )
+    for r in range(rows_here):
+        for c in range(cols_here):
+            padded[r + 1, c + 1] = field_ref[r, c]
 
     def run_rows(at):
         return pl.ds(pl.multiple_of(at * planes * tile, planes * tile), planes * tile)
@@ -301,38 +330,46 @@
         weights_high[b], weights_low[b] = two(weights[b])
         back_near[b, near_count] = jnp.zeros((chains, sites), jnp.float32)
 
+    arrived(5, 1)
+    for e in (0, far_r):
+        send(padded.at[e, cols_here], padded.at[e, 0], 22, w, right)
+        send(padded.at[e, 1], padded.at[e, far_c], 22, w, left)
+
     pltpu.make_async_copy(other_runs, other_runs, sem(17)).wait()
-    other_picks = picks.at[pl.ds(0, GROUP - 1)]
+    other_picks = picks.at[pl.ds(0, SLICES - 1)]
     pltpu.make_async_copy(other_picks, other_picks, sem(3)).wait()
     held = jnp.concatenate(
         [slices[pl.ds(r, coarse_total, stride=piece), :] for r in range(piece)], axis=1
     )
-    pick = jnp.concatenate([picks[s] for s in range(GROUP)], axis=0).astype(jnp.bfloat16)
+    for e, (dy, dz, _) in enumerate(AROUND):
+        first, count = taken(-dy, -dz)
+        for q in range(count):
+            row = (STARTS[e] + q) * quarter
+            all_picks[row : row + quarter, :] = picks[e, first + q, :quarter, :]
+    pick = all_picks[...].astype(jnp.bfloat16)
     chosen = dot_pick(pick, held, NN)
     for r in range(piece):
-        far_send[pl.ds(r, GROUP * reads, stride=piece), :] = chosen[:, r * sites : (r + 1) * sites]
-
-    def group_rows(s):
-        return pl.ds(pl.multiple_of(s * message, message), message)
-
-    def exchange(source, target, send_sem, recv_sem):
-        pltpu.make_async_copy(
-            source.at[group_rows(mine)], target.at[group_rows(mine)], recv_sem
-        ).start()
-        for to_w, to_n, s in members:
-            pltpu.make_async_remote_copy(
-                src_ref=source.at[group_rows(s)],
-                dst_ref=target.at[group_rows(mine)],
-                send_sem=send_sem,
-                recv_sem=recv_sem,
-                device_id=(to_w, to_n),
-                device_id_type=MESH,
-            ).start()
-
-    exchange(far_send, far_recv, sem(6), sem(7))
-
-    interior = padded.at[pl.ds(0, 4)]
-    pltpu.make_async_copy(interior, interior, sem(5)).wait()
+        far_send[pl.ds(r, SLICES * reads, stride=piece), :] = chosen[:, r * sites : (r + 1) * sites]
+
+    rows_part = quarter * piece
+
+    def by_slice(ref, s, first, count):
+        row = pl.multiple_of(s * message + first * rows_part, rows_part)
+        return ref.at[pl.ds(row, count * rows_part)]
+
+    def by_device(ref, e, count):
+        return ref.at[pl.ds(STARTS[e] * rows_part, count * rows_part)]
+
+    pltpu.make_async_copy(
+        by_device(far_send, 0, PARTS), by_slice(far_recv, mine, 0, PARTS), sem(7)
+    ).start()
+    for e in range(1, len(AROUND)):
+        (dy, dz, _), (to_w, to_n, _) = AROUND[e], members[e]
+        first, count = taken(-dy, -dz)
+        send(by_device(far_send, e, count), by_slice(far_recv, mine, first, count), 6, to_w, to_n)
+
+    arrived(21, 2)
+    arrived(23, 1)
     width = cols_here + 2
     for b in range(blocks):
         r, c = b // cols_here, b % cols_here
@@ -367,7 +404,15 @@
                 terms_send[s * message + i * piece : s * message + (i + 1) * piece, :] = back[
                     s * piece : (s + 1) * piece, j * sites : (j + 1) * sites
                 ]
-    exchange(terms_send, terms_recv, sem(8), sem(9))
+    pltpu.make_async_copy(
+        by_slice(terms_send, mine, 0, PARTS), by_device(terms_recv, 0, PARTS), sem(9)
+    ).start()
+    for (dy, dz, dc), (to_w, to_n, s) in zip(AROUND[1:], members[1:]):
+        first, count = taken(dy, dz)
+        there = AROUND.index((-dy, -dz, dc))
+        send(
+            by_slice(terms_send, s, first, count), by_device(terms_recv, there, count), 8, to_w, to_n
+        )
 
     for b in range(blocks):
         back = dot_split(
@@ -390,20 +435,15 @@
                 term = back_near[b, slot]
                 total = term if total is None else total + term
             rim[pr, pc] = total
-    for dr, dc in PLACES:
-        to_w, to_n = row_spans[dr][1], col_spans[dc][1]
-        pltpu.make_async_remote_copy(
-            src_ref=rim.at[rim_rows[dr], rim_cols[dc]],
-            dst_ref=rim_in.at[rim_rows[-dr], rim_cols[-dc]],
-            send_sem=sem(10),
-            recv_sem=sem(11),
-            device_id=(to_w, to_n),
-            device_id_type=MESH,
-        ).start()
+    for e in (0, far_r):
+        send(rim.at[e, far_c], rim_in.at[e, 0], 10, w, right)
+        send(rim.at[e, 0], rim_in.at[e, far_c], 10, w, left)
+    send(rim.at[rows_mid, far_c], rim_in.at[rows_mid, 0], 24, w, right)
+    send(rim.at[rows_mid, 0], rim_in.at[rows_mid, far_c], 24, w, left)
 
     pltpu.make_async_copy(terms_recv, terms_recv, sem(9)).wait()
     gathered = jnp.concatenate(
-        [terms_recv[pl.ds(r, GROUP * reads, stride=piece), :] for r in range(piece)], axis=1
+        [terms_recv[pl.ds(r, SLICES * reads, stride=piece), :] for r in range(piece)], axis=1
     )
     summed = dot_pick(pick, gathered, TN)
     for r in range(piece):
@@ -419,6 +459,14 @@
             device_id=(plane * RUN + beside(t), n),
             device_id_type=MESH,
         ).start()
+
+    arrived(11, 1)
+    for e in (0, far_r):
+        rim[e, 1] = rim[e, 1] + rim_in[e, 0]
+        rim[e, cols_here] = rim[e, cols_here] + rim_in[e, far_c]
+    send(rim.at[far_r, cols_mid], rim_in.at[0, cols_mid], 26, up, n)
+    send(rim.at[0, cols_mid], rim_in.at[far_r, cols_mid], 26, down, n)
+
     pltpu.make_async_copy(sums_beside, sums_beside, sem(19)).wait()
     plane_sums[...] = jnp.sum(sums_beside[...], axis=0).reshape(planes, tile, sites)
     pltpu.make_async_copy(plane_sums.at[plane], sums_in.at[plane], sem(13)).start()
@@ -429,27 +477,24 @@
             dst_ref=sums_in.at[plane],
             send_sem=sem(12),
             recv_sem=sem(13),
-            device_id=(across(t) * RUN + x, n),
+            device_id=(across(t) * RUN + x, column(across(t))),
             device_id_type=MESH,
         ).start()
         return carry
 
     lax.fori_loop(1, planes, send_sums, 0)
 
-    around = rim_in.at[pl.ds(0, 4)]
-    pltpu.make_async_copy(around, around, sem(11)).wait()
+    arrived(25, 2)
+    arrived(27, 1)
     for r in range(rows_here):
         for c in range(cols_here):
             total = fine_out[r, c] - back_white[r * cols_here + c] + rim[r + 1, c + 1]
-            edge_r = [e for e, at in ((0, 0), (last_r + 1, rows_here - 1)) if r == at]
-            edge_c = [e for e, at in ((0, 0), (last_c + 1, cols_here - 1)) if c == at]
-            for e in edge_r:
-                total = total + rim_in[e, c + 1]
-            for f in edge_c:
-                total = total + rim_in[r + 1, f]
-            for e in edge_r:
-                for f in edge_c:
-                    total = total + rim_in[e, f]
+            for e, at in ((0, 0), (far_r, rows_here - 1)):
+                if r == at:
+                    total = total + rim_in[e, c + 1]
+            for e, at in ((0, 0), (far_c, cols_here - 1)):
+                if c == at:
+                    total = total + rim_in[r + 1, e]
             fine_out[r, c] = total
 
     pltpu.make_async_copy(sums_in, sums_in, sem(13)).wait()
@@ -481,11 +526,11 @@
     pltpu.make_async_copy(other_runs, other_runs, sem(16)).wait()
     pltpu.make_async_copy(other_runs, other_runs, sem(18)).wait()
     pltpu.make_async_copy(other_picks, other_picks, sem(2)).wait()
-    pltpu.make_async_copy(interior, interior, sem(4)).wait()
-    others = far_send.at[pl.ds(0, (GROUP - 1) * message)]
+    others = far_send.at[pl.ds(0, (SLICES - 1) * message)]
     pltpu.make_async_copy(others, others, sem(6)).wait()
     pltpu.make_async_copy(others, others, sem(8)).wait()
-    pltpu.make_async_copy(around, around, sem(10)).wait()
+    for i, rows in ((4, 1), (20, 2), (22, 1), (10, 1), (24, 2), (26, 1)):
+        arrived(i, rows)
     pltpu.make_async_copy(sent, sent, sem(12)).wait()
 
     pltpu.make_async_copy(other_totals, other_totals, sem(14)).wait()
@@ -552,15 +597,16 @@
             pltpu.VMEM((rows_here + 2, cols_here + 2, chains, sites), f32),
             pltpu.VMEM((SLICES, owned * piece, sites), f32),
             pltpu.VMEM((wide_count * owned * piece, sites), f32),
-            pltpu.VMEM((GROUP, reads, wide_count * owned), f32),
-            pltpu.VMEM((GROUP * reads * piece, sites), f32),
-            pltpu.VMEM((GROUP * reads * piece, sites), f32),
+            pltpu.VMEM((len(AROUND), PARTS, 8, wide_count * owned), f32),
+            pltpu.VMEM((reads * SLICES, wide_count * owned), f32),
+            pltpu.VMEM((SLICES * reads * piece, sites), f32),
+            pltpu.VMEM((SLICES * reads * piece, sites), f32),
             pltpu.VMEM((reads, chains, sites), f32),
             pltpu.VMEM((blocks, near_count + 1, chains, sites), f32),
             pltpu.VMEM((blocks, chains, sites), f32),
             pltpu.VMEM((blocks, chains, sites), f32),
-            pltpu.VMEM((GROUP * reads * piece, sites), f32),
-            pltpu.VMEM((GROUP * reads * piece, sites), f32),
+            pltpu.VMEM((SLICES * reads * piece, sites), f32),
+            pltpu.VMEM((SLICES * reads * piece, sites), f32),
             pltpu.VMEM((wide_count * owned * piece, sites), f32),
             pltpu.VMEM((RUN, wide_count // RUN * owned * piece, sites), f32),
             pltpu.VMEM((wide_count // RUN, owned * piece, sites), f32),
@@ -568,7 +614,7 @@
             pltpu.VMEM((narrow_count, 2, owned * piece, sites), f32),
             pltpu.SMEM((blocks * near_count,), jnp.int32),
             pltpu.SemaphoreType.DMA((blocks,)),
-            pltpu.SemaphoreType.DMA((20,)),
+            pltpu.SemaphoreType.DMA((28,)),
             pltpu.SemaphoreType.DMA((len(operands),)),
         ],
         compiler_params=pltpu.CompilerParams(

time: 63.9 us -> 61.3 us (0.959)
  Pallas kernels: 61.8 us -> 59.2 us
    pallas_call x1, Pallas kernels: 61.8 us -> 59.2 us  [per_device(): pl.pallas_call(functools.partial(kernel, wide_count, narrow_count), out_s...]
where the time goes in v3:
time: 61.3 us; the launch traced here: 61.1 us
  Pallas kernels  59.2 us (97%)
  local copies, waits for them, and re-layouts  1.27 us (2%)
  between operations  0.64 us (1%)
    pallas_call x1, Pallas kernels, per_device(): pl.pallas_call(functools.partial(kernel, wide_count, narrow_count), out_s...  59.2 us
    unnamed x2, local copies, waits for them, and re-layouts  1.27 us

profile of v3, /device:TPU:1, one launch (start us, length us, event | category | flops | bytes accessed | tf_op | source)
XLA Modules:
  0.0 61.1 jit_solution(4744406608731827642)
XLA Ops:
  0.6 59.2 %shard_map.131 = (f32[4,2,32,128]{3,2,1,0:T(8,128)S(1)}, f32[2,32,128]{2,1,0:T(8,128)S(1)}) custom-call(f32[8,128,896]{2,1,0:T(8,128)} %bitcast.5, f32[4,2,32,128]{3,2,1,0:T(8,128)} %refs_0_.1, s32[8,128]{1,0:T(8,128)} %bitcast.7, f32[8,128]{1,0:T(8,128)} %bitcast.8, f32[8,128,128]{2,1,0:T(8,128)} %bitcast.6, s32[4,2,4]{2,1,0:T(2,128)} %refs_4_.1, ...), custom_call_target="tpu_custom_call" | custom-call | tf_op jit(solution)/shard_map/pallas_call | solution.py:577
  59.9 0.7 %copy.16 = f32[4,2,32,128]{3,2,1,0:T(8,128)} copy(f32[4,2,32,128]{3,2,1,0:T(8,128)S(1)} %get-tuple-element.2) | data formatting | bytes 262144
  60.5 0.6 %copy.17 = f32[2,32,128]{2,1,0:T(8,128)} copy(f32[2,32,128]{2,1,0:T(8,128)S(1)} %get-tuple-element.3) | data formatting | bytes 65536

commit v4 on v3

--- a/solution.py
+++ b/solution.py
@@ -92,6 +92,9 @@
         weights_low,
         gain_high,
         gain_low,
+        gains,
+        reach_high,
+        reach_low,
         padded,
         rim,
         rim_in,
@@ -157,6 +160,12 @@
     up, down = lax.rem(w + 1, wide_count), lax.rem(w + wide_count - 1, wide_count)
     right, left = lax.rem(n + 1, narrow_count), lax.rem(n + narrow_count - 1, narrow_count)
 
+    copies = {
+        i: pltpu.make_async_copy(inputs[i], held_here[i], copy_sems.at[i])
+        for i in range(len(inputs))
+    }
+    copies[7].start()
+
     barrier = pltpu.get_barrier_semaphore()
 
     def greet(to_w, to_n):
@@ -186,9 +195,7 @@
     greet(down, n)
     greetings = planes - 1 + RUN - 1 + narrow_count - 1 + len(AROUND) - 1 + 2
 
-    copies = {}
-    for i in (7, 4, 5, 6, 0, 1, 2, 8, 9, 10, 3):
-        copies[i] = pltpu.make_async_copy(inputs[i], held_here[i], copy_sems.at[i])
+    for i in (0, 4, 5, 6, 1, 2, 8, 9, 10, 3):
         copies[i].start()
     weight_copies = [
         pltpu.make_async_copy(kriging_ref.at[b], weights.at[b], weight_sems.at[b])
@@ -308,6 +315,7 @@
         gain = lax.dot_general(
             whiten_ref[b], whiten_ref[b], TN, precision=EXACT, preferred_element_type=jnp.float32
         )
+        gains[b] = gain
         gain_high[b], gain_low[b] = two(gain)
     for j in range(owned):
         white = lax.dot_general(
@@ -328,6 +336,8 @@
         )
         weight_copies[b].wait()
         weights_high[b], weights_low[b] = two(weights[b])
+        reach = dot_split(gains[b], weights_high[b, :, near_sites:], weights_low[b, :, near_sites:], NN)
+        reach_high[b], reach_low[b] = two(reach)
         back_near[b, near_count] = jnp.zeros((chains, sites), jnp.float32)
 
     arrived(5, 1)
@@ -390,14 +400,11 @@
             ]
     for b in range(blocks):
         distant = jnp.concatenate([far[b * far_count + j] for j in range(far_count)], axis=1)
-        left_over = resid[b] - dot_split(
+        resid[b] = resid[b] - dot_split(
             distant, weights_high[b, :, near_sites:], weights_low[b, :, near_sites:], NT
         )
-        back_white[b] = dot_split(left_over, gain_high[b], gain_low[b], NN)
-    for b in range(blocks):
-        back = dot_split(
-            back_white[b], weights_high[b, :, near_sites:], weights_low[b, :, near_sites:], NN
-        )
+    for b in range(blocks):
+        back = dot_split(resid[b], reach_high[b], reach_low[b], NN)
         for j in range(far_count):
             i = b * far_count + j
             for s in range(SLICES):
@@ -414,6 +421,8 @@
             by_slice(terms_send, s, first, count), by_device(terms_recv, there, count), 8, to_w, to_n
         )
 
+    for b in range(blocks):
+        back_white[b] = dot_split(resid[b], gain_high[b], gain_low[b], NN)
     for b in range(blocks):
         back = dot_split(
             back_white[b], weights_high[b, :, :near_sites], weights_low[b, :, :near_sites], NN
@@ -592,6 +601,9 @@
             pltpu.VMEM((blocks, sites, cond), bf16),
             pltpu.VMEM((blocks, sites, sites), bf16),
             pltpu.VMEM((blocks, sites, sites), bf16),
+            pltpu.VMEM((blocks, sites, sites), f32),
+            pltpu.VMEM((blocks, sites, far_count * sites), bf16),
+            pltpu.VMEM((blocks, sites, far_count * sites), bf16),
             pltpu.VMEM((rows_here + 2, cols_here + 2, chains, sites), f32),
             pltpu.VMEM((rows_here + 2, cols_here + 2, chains, sites), f32),
             pltpu.VMEM((rows_here + 2, cols_here + 2, chains, sites), f32),

time: 61.3 us -> 60.3 us (0.984)
  Pallas kernels: 59.2 us -> 58.2 us
    pallas_call x1, Pallas kernels: 59.2 us -> 58.2 us  [per_device(): pl.pallas_call(functools.partial(kernel, wide_count, narrow_count), out_s...]
where the time goes in v4:
time: 60.3 us; the launch traced here: 60.1 us
  Pallas kernels  58.2 us (97%)
  local copies, waits for them, and re-layouts  1.27 us (2%)
  between operations  0.64 us (1%)
    pallas_call x1, Pallas kernels, per_device(): pl.pallas_call(functools.partial(kernel, wide_count, narrow_count), out_s...  58.2 us
    unnamed x2, local copies, waits for them, and re-layouts  1.27 us

profile of v4, /device:TPU:1, one launch (start us, length us, event | category | flops | bytes accessed | tf_op | source)
XLA Modules:
  0.0 60.1 jit_solution(13409466337263826871)
XLA Ops:
  0.6 58.2 %shard_map.131 = (f32[4,2,32,128]{3,2,1,0:T(8,128)S(1)}, f32[2,32,128]{2,1,0:T(8,128)S(1)}) custom-call(f32[8,128,896]{2,1,0:T(8,128)} %bitcast.5, f32[4,2,32,128]{3,2,1,0:T(8,128)} %refs_0_.1, s32[8,128]{1,0:T(8,128)} %bitcast.7, f32[8,128]{1,0:T(8,128)} %bitcast.8, f32[8,128,128]{2,1,0:T(8,128)} %bitcast.6, s32[4,2,4]{2,1,0:T(2,128)} %refs_4_.1, ...), custom_call_target="tpu_custom_call" | custom-call | tf_op jit(solution)/shard_map/pallas_call | solution.py:586
  58.8 0.7 %copy.16 = f32[4,2,32,128]{3,2,1,0:T(8,128)} copy(f32[4,2,32,128]{3,2,1,0:T(8,128)S(1)} %get-tuple-element.2) | data formatting | bytes 262144
  59.5 0.6 %copy.17 = f32[2,32,128]{2,1,0:T(8,128)} copy(f32[2,32,128]{2,1,0:T(8,128)S(1)} %get-tuple-element.3) | data formatting | bytes 65536

commit v5 on v4

--- a/solution.py
+++ b/solution.py
@@ -172,7 +172,7 @@
         pl.semaphore_signal(barrier, inc=1, device_id=(to_w, to_n), device_id_type=MESH)
 
     def across(t):
-        return lax.rem(plane + t, planes)
+        return lax.rem(plane + 1 + lax.rem(t + planes // 2 - 2, planes - 1), planes)
 
     def beside(t):
         return lax.rem(x + t, RUN)
@@ -185,7 +185,7 @@
         return carry
 
     lax.fori_loop(1, planes, greet_planes, 0)
-    for t in range(1, RUN):
+    for t in (2, 1, 3):
         greet(plane * RUN + beside(t), n)
     for t in range(1, narrow_count):
         greet(w, lax.rem(n + t, narrow_count))
@@ -283,7 +283,7 @@
 
     gathered_here = slices.at[run_rows(x)]
     pltpu.make_async_copy(gathered_here, gathered_here, sem(1)).wait()
-    for t in range(1, RUN):
+    for t in (2, 1, 3):
         pltpu.make_async_remote_copy(
             src_ref=gathered_here,
             dst_ref=gathered_here,
@@ -373,7 +373,7 @@
     pltpu.make_async_copy(
         by_device(far_send, 0, PARTS), by_slice(far_recv, mine, 0, PARTS), sem(7)
     ).start()
-    for e in range(1, len(AROUND)):
+    for e in reversed(range(1, len(AROUND))):
         (dy, dz, _), (to_w, to_n, _) = AROUND[e], members[e]
         first, count = taken(-dy, -dz)
         send(by_device(far_send, e, count), by_slice(far_recv, mine, first, count), 6, to_w, to_n)
@@ -414,7 +414,7 @@
     pltpu.make_async_copy(
         by_slice(terms_send, mine, 0, PARTS), by_device(terms_recv, 0, PARTS), sem(9)
     ).start()
-    for (dy, dz, dc), (to_w, to_n, s) in zip(AROUND[1:], members[1:]):
+    for (dy, dz, dc), (to_w, to_n, s) in zip(AROUND[:0:-1], members[:0:-1]):
         first, count = taken(dy, dz)
         there = AROUND.index((-dy, -dz, dc))
         send(
@@ -459,7 +459,7 @@
         sums[pl.ds(r, coarse_total, stride=piece), :] = summed[:, r * sites : (r + 1) * sites]
 
     pltpu.make_async_copy(sums.at[run_rows(x)], sums_beside.at[x], sem(19)).start()
-    for t in range(1, RUN):
+    for t in (2, 1, 3):
         pltpu.make_async_remote_copy(
             src_ref=sums.at[run_rows(beside(t))],
             dst_ref=sums_beside.at[x],

time: 60.3 us -> 57.5 us (0.954)
  Pallas kernels: 58.2 us -> 55.4 us
    pallas_call x1, Pallas kernels: 58.2 us -> 55.4 us  [per_device(): pl.pallas_call(functools.partial(kernel, wide_count, narrow_count), out_s...]
where the time goes in v5:
time: 57.5 us; the launch traced here: 57.3 us
  Pallas kernels  55.4 us (96%)
  local copies, waits for them, and re-layouts  1.27 us (2%)
  between operations  0.64 us (1%)
    pallas_call x1, Pallas kernels, per_device(): pl.pallas_call(functools.partial(kernel, wide_count, narrow_count), out_s...  55.4 us
    unnamed x2, local copies, waits for them, and re-layouts  1.27 us

profile of v5, /device:TPU:1, one launch (start us, length us, event | category | flops | bytes accessed | tf_op | source)
XLA Modules:
  0.0 57.3 jit_solution(14676162995213670303)
XLA Ops:
  0.6 55.4 %shard_map.131 = (f32[4,2,32,128]{3,2,1,0:T(8,128)S(1)}, f32[2,32,128]{2,1,0:T(8,128)S(1)}) custom-call(f32[8,128,896]{2,1,0:T(8,128)} %bitcast.5, f32[4,2,32,128]{3,2,1,0:T(8,128)} %refs_0_.1, s32[8,128]{1,0:T(8,128)} %bitcast.7, f32[8,128]{1,0:T(8,128)} %bitcast.8, f32[8,128,128]{2,1,0:T(8,128)} %bitcast.6, s32[4,2,4]{2,1,0:T(2,128)} %refs_4_.1, ...), custom_call_target="tpu_custom_call" | custom-call | tf_op jit(solution)/shard_map/pallas_call | solution.py:586
  56.1 0.7 %copy.16 = f32[4,2,32,128]{3,2,1,0:T(8,128)} copy(f32[4,2,32,128]{3,2,1,0:T(8,128)S(1)} %get-tuple-element.2) | data formatting | bytes 262144
  56.7 0.6 %copy.17 = f32[2,32,128]{2,1,0:T(8,128)} copy(f32[2,32,128]{2,1,0:T(8,128)S(1)} %get-tuple-element.3) | data formatting | bytes 65536
